TPU v7x, 32 devices: a whole 2x2x4 slice. The times are simulated.
32 devices in a mesh: dp: 16 (over z, x, core), tensor: 2 (over y).
Axes of the slice: x: 2, y: 2, z: 4, core: 2. Of those that a mesh axis runs over, the one named last changes fastest.
Arguments:
- tokens: bfloat16 [16384, 1024], P('dp'), may hold values from -6 to 6
- out_grad: bfloat16 [16384, 1024], P('dp'), may hold values from -6 to 6
- segment_ids: int32 [16384], P('dp'), may hold values from -1 to 31, as said below
- norm_gains: float32 [2, 1024], replicated, may hold values from 0.25 to 1.75
- w_zx: bfloat16 [1024, 2, 1536], P(None, None, 'tensor'), may hold values from -0.1875 to 0.1875
- w_bc: bfloat16 [1024, 256], replicated, may hold values from -0.1875 to 0.1875
- w_dt: bfloat16 [1024, 24], P(None, 'tensor'), may hold values from -0.1875 to 0.1875
- conv_x: float32 [5, 1536], P(None, 'tensor'), may hold values from -3 to 3
- conv_bc: float32 [5, 256], replicated, may hold values from -3 to 3
- head_params: float32 [3, 24], P(None, 'tensor'), may hold values from -4 to 1.5
- ssm_gain: float32 [1536], P('tensor'), may hold values from 0.25 to 1.75
- w_out: bfloat16 [1536, 1024], P('tensor'), may hold values from -0.15625 to 0.15625
- w_q: bfloat16 [1024, 512], P(None, 'tensor'), may hold values from -0.1875 to 0.1875
- w_kv: bfloat16 [1024, 2, 128], P(None, None, 'tensor'), may hold values from -0.1875 to 0.1875
- w_o: bfloat16 [512, 1024], P('tensor'), may hold values from -6 to 6
- w_gate_up: bfloat16 [1024, 2, 2048], P(None, None, 'tensor'), may hold values from -0.1875 to 0.1875
- w_down: bfloat16 [2048, 1024], P('tensor'), may hold values from -0.125 to 0.125
Outputs:
- mixed: bfloat16 [16384, 1024], P('dp')
- grad_tokens: float32 [16384, 1024], P('dp')
- grad_norm_gains: float32 [2, 1024], P(None, ('dp', 'tensor'))
- grad_w_zx: float32 [1024, 2, 1536], P('dp', None, 'tensor')
- grad_w_bc: float32 [1024, 256], P(('dp', 'tensor'))
- grad_w_dt: float32 [1024, 24], P('dp', 'tensor')
- grad_conv_x: float32 [5, 1536], P(None, 'tensor')
- grad_conv_bc: float32 [5, 256], P(None, ('dp', 'tensor'))
- grad_head_params: float32 [3, 24], P(None, 'tensor')
- grad_ssm_gain: float32 [1536], P('tensor')
- grad_w_out: float32 [1536, 1024], P('tensor', 'dp')
- grad_w_q: float32 [1024, 512], P('dp', 'tensor')
- grad_w_kv: float32 [1024, 2, 128], P('dp', None, 'tensor')
- grad_w_o: float32 [512, 1024], P('tensor', 'dp')
- grad_w_gate_up: float32 [1024, 2, 2048], P('dp', None, 'tensor')
- grad_w_down: float32 [2048, 1024], P('tensor', 'dp')
Inputs may be any that keep to these rules, and one draw needn't show every extreme that they name: `segment_ids`: equal numbers form contiguous runs inside one block of 1024 slots and rise along the slots; -1 marks empty slots at a block's end; each sequence has 512 to 1024 tokens, each block holds one or two sequences, and some block is full.
All inputs are finite; a program needn't handle non-finite values.
Results may differ from a plain program's by a relative error of at most 0.012.
Values sent between devices are 32-bit elements; how exact they have to be, the bound alone decides.
A program may use at most 256 MiB of HBM per device.

v0:
```python
import math

import jax
import jax.numpy as jnp
from jax import lax
from jax.sharding import PartitionSpec as P

SSM_HEAD_DIM = 64
ATT_HEAD_DIM = 64
SPAN = 128
INNER = 1536


EPS = 1e-05
ROPE_BASE = 100000000000.0


def product(left, right):
    return jnp.dot(left, right, preferred_element_type=jnp.float32)


def product_back(left, right):
    return lax.dot_general(
        left, right, (((1,), (1,)), ((), ())), preferred_element_type=jnp.float32
    )


def weight_product(left, right):
    return lax.dot_general(
        left, right, (((0,), (0,)), ((), ())), preferred_element_type=jnp.float32
    )


def norm_scale(values):
    return lax.rsqrt(jnp.mean(values * values, axis=-1, keepdims=True) + EPS)


def norm_back(grad_normed, unit, scale, gain):
    grad_unit = grad_normed * gain[None, :]
    return scale * (grad_unit - unit * jnp.mean(grad_unit * unit, axis=-1, keepdims=True))


def token_places(segments):
    count = segments.shape[0]
    index = jnp.arange(count, dtype=jnp.int32)
    starts = jnp.concatenate([jnp.ones((1,), dtype=bool), segments[1:] != segments[:-1]])
    first = lax.cummax(jnp.where(starts, index, 0), axis=0)
    return (index - first).astype(jnp.float32)


def rotary_tables(places, head_dim):
    half = head_dim // 2
    freqs = jnp.exp(jnp.arange(half, dtype=jnp.float32) * (-2.0 * math.log(ROPE_BASE) / head_dim))
    angle = places[:, None] * freqs[None, :]
    return (jnp.cos(angle), jnp.sin(angle))


def rotate(values, cosines, sines):
    half = values.shape[-1] // 2
    first = values[..., :half]
    second = values[..., half:]
    cosines = cosines[:, None, :]
    sines = sines[:, None, :]
    return jnp.concatenate(
        [first * cosines - second * sines, second * cosines + first * sines], axis=-1
    )


def rotate_back(grads, cosines, sines):
    half = grads.shape[-1] // 2
    first = grads[..., :half]
    second = grads[..., half:]
    cosines = cosines[:, None, :]
    sines = sines[:, None, :]
    return jnp.concatenate(
        [first * cosines + second * sines, second * cosines - first * sines], axis=-1
    )


def causal_filter(values, taps, segments):
    total = values.shape[0]
    width = taps.shape[0] - 1
    result = taps[width][None, :] + taps[0][None, :] * values
    for offset in range(1, width):
        earlier = jnp.concatenate(
            [jnp.zeros((offset, values.shape[1]), values.dtype), values[: total - offset]]
        )
        earlier_seg = jnp.concatenate(
            [jnp.full((offset,), -2, jnp.int32), segments[: total - offset]]
        )
        result = (
            result
            + jnp.where((earlier_seg == segments)[:, None], earlier, 0.0) * taps[offset][None, :]
        )
    return result


def state_space(inputs, steps, rates, b_mat, c_mat, segments):
    total, heads, head_dim = inputs.shape
    nstate = b_mat.shape[1]
    count = total // SPAN
    x_blocks = inputs.reshape(count, SPAN, heads, head_dim)
    step_blocks = steps.reshape(count, SPAN, heads)
    b_blocks = b_mat.reshape(count, SPAN, nstate)
    c_blocks = c_mat.reshape(count, SPAN, nstate)
    seg_blocks = segments.reshape(count, SPAN)
    decay_sum = jnp.cumsum(-step_blocks * rates[None, None, :], axis=1)
    inside = (seg_blocks[:, :, None] == seg_blocks[:, None, :]) & jnp.tril(
        jnp.ones((SPAN, SPAN), dtype=bool)
    )[None]
    inside = inside[..., None]
    gap = decay_sum[:, :, None, :] - decay_sum[:, None, :, :]
    weights = jnp.exp(jnp.where(inside, gap, 0.0)) * inside.astype(jnp.float32)
    intersection = jnp.einsum("cin,cjn->cij", c_blocks, b_blocks, precision=lax.Precision.HIGHEST)
    weights = weights * intersection[..., None] * step_blocks[:, None, :, :]
    within = jnp.einsum("cijh,cjhp->cihp", weights, x_blocks, precision=lax.Precision.HIGHEST)
    last_seg = seg_blocks[:, -1]
    final = decay_sum[:, -1, :]
    tail = (
        (seg_blocks == last_seg[:, None]).astype(jnp.float32)[:, :, None]
        * jnp.exp(final[:, None, :] - decay_sum)
        * step_blocks
    )
    block_state = jnp.einsum(
        "cjh,cjhp,cjn->chpn", tail, x_blocks, b_blocks, precision=lax.Precision.HIGHEST
    )
    carry_on = jnp.concatenate(
        [jnp.zeros((1,), jnp.float32), (last_seg[1:] == last_seg[:-1]).astype(jnp.float32)]
    )
    factor = jnp.exp(final) * carry_on[:, None]

    def advance(state, pair):
        new_state = pair[0][:, None, None] * state + pair[1]
        return (new_state, state)

    unused, entering = lax.scan(
        advance, jnp.zeros((heads, head_dim, nstate), jnp.float32), (factor, block_state)
    )
    previous = jnp.concatenate([jnp.full((1,), -3, jnp.int32), last_seg[:-1]])
    head_weight = (seg_blocks == previous[:, None]).astype(jnp.float32)[:, :, None] * jnp.exp(
        decay_sum
    )
    carried = (
        jnp.einsum("cin,chpn->cihp", c_blocks, entering, precision=lax.Precision.HIGHEST)
        * head_weight[..., None]
    )
    return (within + carried).reshape(total, heads, head_dim)


def mixer_core(gate_and_x, step_raw, state_maps, conv_x, conv_bc, head_params, segments):
    total = gate_and_x.shape[0]
    heads = step_raw.shape[1]
    z_part = gate_and_x[:, 0]
    x_part = jax.nn.silu(causal_filter(gate_and_x[:, 1], conv_x, segments))
    maps = jax.nn.silu(causal_filter(state_maps, conv_bc, segments))
    nstate = state_maps.shape[1] // 2
    x_heads = x_part.reshape(total, heads, SSM_HEAD_DIM)
    rates = jnp.exp(head_params[0])
    steps = jax.nn.softplus(step_raw + head_params[1][None, :])
    output = state_space(x_heads, steps, rates, maps[:, :nstate], maps[:, nstate:], segments)
    output = output + head_params[2][None, :, None] * x_heads
    return output.reshape(total, heads * SSM_HEAD_DIM) * jax.nn.silu(z_part)


def block_scores(part, keys, segments, start, block, index, scale):
    part_seg = lax.dynamic_slice_in_dim(segments, start, block, 0)
    scores = jnp.einsum("ikgd,jkd->kgij", part, keys, preferred_element_type=jnp.float32) * scale
    rows_here = start + jnp.arange(block, dtype=jnp.int32)
    allowed = (part_seg[:, None] == segments[None, :]) & (rows_here[:, None] >= index[None, :])
    return jnp.where(allowed[None, None], scores, -1e30)


def attend(queries, keys, values, segments):
    total = queries.shape[0]
    block = min(512, total)
    scale = queries.shape[-1] ** (-0.5)
    index = jnp.arange(total, dtype=jnp.int32)

    def one_block(number):
        start = number * block
        part = lax.dynamic_slice_in_dim(queries, start, block, 0)
        scores = block_scores(part, keys, segments, start, block, index, scale)
        log_sum = jax.nn.logsumexp(scores, axis=-1)
        probs = jnp.exp(scores - log_sum[..., None]).astype(jnp.bfloat16)
        return (
            jnp.einsum("kgij,jkd->ikgd", probs, values, preferred_element_type=jnp.float32),
            log_sum,
        )

    outputs, log_sums = lax.map(one_block, jnp.arange(total // block, dtype=jnp.int32))
    return (outputs.reshape(queries.shape), log_sums)


def attend_back(queries, keys, values, segments, log_sums, grad_out):
    total = queries.shape[0]
    block = min(512, total)
    scale = queries.shape[-1] ** (-0.5)
    index = jnp.arange(total, dtype=jnp.int32)

    def one_step(carry, number):
        grad_keys, grad_values = carry
        start = number * block
        part = lax.dynamic_slice_in_dim(queries, start, block, 0)
        part_grad = lax.dynamic_slice_in_dim(grad_out, start, block, 0)
        scores = block_scores(part, keys, segments, start, block, index, scale)
        probs = jnp.exp(scores - log_sums[number][..., None])
        grad_probs = jnp.einsum(
            "ikgd,jkd->kgij", part_grad, values, preferred_element_type=jnp.float32
        )
        grad_scores = (
            probs * (grad_probs - jnp.sum(probs * grad_probs, axis=-1, keepdims=True))
        ).astype(jnp.bfloat16)
        grad_part = (
            jnp.einsum("kgij,jkd->ikgd", grad_scores, keys, preferred_element_type=jnp.float32)
            * scale
        )
        grad_keys = (
            grad_keys
            + jnp.einsum("kgij,ikgd->jkd", grad_scores, part, preferred_element_type=jnp.float32)
            * scale
        )
        grad_values = grad_values + jnp.einsum(
            "kgij,ikgd->jkd",
            probs.astype(jnp.bfloat16),
            part_grad,
            preferred_element_type=jnp.float32,
        )
        return ((grad_keys, grad_values), grad_part)

    zeros = jnp.zeros(keys.shape, jnp.float32)
    sums, grad_parts = lax.scan(
        one_step, (zeros, zeros), jnp.arange(total // block, dtype=jnp.int32)
    )
    return (grad_parts.reshape(queries.shape), sums[0], sums[1])


def on_device(
    tokens,
    out_grad,
    segment_ids,
    norm_gains,
    w_zx,
    w_bc,
    w_dt,
    conv_x,
    conv_bc,
    head_params,
    ssm_gain,
    w_out,
    w_q,
    w_kv,
    w_o,
    w_gate_up,
    w_down,
):
    total, width = tokens.shape
    inner_local = w_zx.shape[2]
    hidden_local = w_gate_up.shape[2]
    key_heads = w_kv.shape[2] // ATT_HEAD_DIM
    query_heads = w_q.shape[1] // ATT_HEAD_DIM
    group = query_heads // key_heads
    mixer_weight = w_zx.reshape(width, 2 * inner_local)
    key_value_weight = w_kv.reshape(width, 2 * key_heads * ATT_HEAD_DIM)
    gate_up_weight = w_gate_up.reshape(width, 2 * hidden_local)
    resid = tokens.astype(jnp.float32)
    live = (segment_ids >= 0).astype(jnp.float32)[:, None]
    cotangent = (out_grad.astype(jnp.float32) * live).astype(jnp.bfloat16)
    scale_in = norm_scale(resid)
    unit_in = resid * scale_in
    normed_in = (unit_in * norm_gains[0][None, :]).astype(jnp.bfloat16)
    gate_and_x = product(normed_in, mixer_weight).reshape(total, 2, inner_local)
    step_raw = product(normed_in, w_dt)
    state_maps = product(normed_in, w_bc)

    def local_mixer(first, second, third, fourth, fifth, sixth):
        return mixer_core(first, second, third, fourth, fifth, sixth, segment_ids)

    gated, mixer_pullback = jax.vjp(
        local_mixer, gate_and_x, step_raw, state_maps, conv_x, conv_bc, head_params
    )
    squares = lax.psum(jnp.sum(gated * gated, axis=1), "tensor")
    scale_ssm = lax.rsqrt(squares[:, None] / INNER + EPS)
    unit_ssm = gated * scale_ssm
    mixed_ssm = (unit_ssm * ssm_gain[None, :]).astype(jnp.bfloat16)
    cosines, sines = rotary_tables(token_places(segment_ids), ATT_HEAD_DIM)
    queries = product(normed_in, w_q).reshape(total, query_heads, ATT_HEAD_DIM)
    key_vals = product(normed_in, key_value_weight).reshape(total, 2, key_heads, ATT_HEAD_DIM)
    queries = (
        rotate(queries, cosines, sines)
        .astype(jnp.bfloat16)
        .reshape(total, key_heads, group, ATT_HEAD_DIM)
    )
    keys = rotate(key_vals[:, 0], cosines, sines).astype(jnp.bfloat16)
    values = key_vals[:, 1].astype(jnp.bfloat16)
    attended, log_sums = attend(queries, keys, values, segment_ids)
    attended = attended.astype(jnp.bfloat16).reshape(total, query_heads * ATT_HEAD_DIM)
    partial_mix = product(mixed_ssm, w_out) + product(attended, w_o)
    middle = resid + lax.psum(partial_mix, "tensor")
    scale_mid = norm_scale(middle)
    unit_mid = middle * scale_mid
    normed_mid = (unit_mid * norm_gains[1][None, :]).astype(jnp.bfloat16)
    gate_up = product(normed_mid, gate_up_weight).reshape(total, 2, hidden_local)
    gate = gate_up[:, 0]
    upper = gate_up[:, 1]
    activation = (jax.nn.silu(gate) * upper).astype(jnp.bfloat16)
    middle_out = middle + lax.psum(product(activation, w_down), "tensor")
    mixed = middle_out.astype(jnp.bfloat16)
    grad_down = weight_product(activation, cotangent)
    delta_act = product_back(cotangent, w_down)
    sigma = jax.nn.sigmoid(gate)
    delta_gate = delta_act * upper * sigma * (1.0 + gate * (1.0 - sigma))
    delta_upper = delta_act * (gate * sigma)
    delta_gate_up = (
        jnp.stack([delta_gate, delta_upper], axis=1)
        .astype(jnp.bfloat16)
        .reshape(total, 2 * hidden_local)
    )
    grad_gate_up = weight_product(normed_mid, delta_gate_up).reshape(width, 2, hidden_local)
    delta_mid_norm = lax.psum(product_back(delta_gate_up, gate_up_weight), "tensor")
    gain_mid = jnp.sum(delta_mid_norm * unit_mid, axis=0)
    delta_middle = norm_back(delta_mid_norm, unit_mid, scale_mid, norm_gains[1]) + cotangent.astype(
        jnp.float32
    )
    delta_mix = delta_middle.astype(jnp.bfloat16)
    grad_out = weight_product(mixed_ssm, delta_mix)
    grad_o = weight_product(attended, delta_mix)
    delta_ssm = product_back(delta_mix, w_out)
    delta_attended = (
        product_back(delta_mix, w_o)
        .astype(jnp.bfloat16)
        .reshape(total, key_heads, group, ATT_HEAD_DIM)
    )
    grad_ssm_gain = jnp.sum(delta_ssm * unit_ssm, axis=0)
    delta_unit = delta_ssm * ssm_gain[None, :]
    across = lax.psum(jnp.sum(delta_unit * gated, axis=1), "tensor")
    delta_gated = scale_ssm * delta_unit - gated * scale_ssm**3 * (across[:, None] / INNER)
    delta_gx, delta_step, delta_maps, grad_conv_x, grad_conv_bc, grad_heads = mixer_pullback(
        delta_gated
    )
    delta_gx = delta_gx.reshape(total, 2 * inner_local).astype(jnp.bfloat16)
    delta_step = delta_step.astype(jnp.bfloat16)
    delta_queries, delta_keys, delta_values = attend_back(
        queries, keys, values, segment_ids, log_sums, delta_attended
    )
    delta_queries = rotate_back(
        delta_queries.reshape(total, query_heads, ATT_HEAD_DIM), cosines, sines
    )
    delta_queries = delta_queries.astype(jnp.bfloat16).reshape(total, query_heads * ATT_HEAD_DIM)
    delta_keys = rotate_back(delta_keys, cosines, sines)
    delta_key_vals = (
        jnp.stack([delta_keys, delta_values], axis=1)
        .astype(jnp.bfloat16)
        .reshape(total, 2 * key_heads * ATT_HEAD_DIM)
    )
    grad_zx = weight_product(normed_in, delta_gx).reshape(width, 2, inner_local)
    grad_dt = weight_product(normed_in, delta_step)
    grad_q = weight_product(normed_in, delta_queries)
    grad_kv = weight_product(normed_in, delta_key_vals).reshape(width, 2, key_heads * ATT_HEAD_DIM)
    grad_bc = lax.dot_general(
        normed_in.astype(jnp.float32),
        delta_maps,
        (((0,), (0,)), ((), ())),
        precision=lax.Precision.HIGHEST,
        preferred_element_type=jnp.float32,
    )
    delta_in_part = (
        product_back(delta_gx, mixer_weight)
        + product_back(delta_step, w_dt)
        + product_back(delta_queries, w_q)
        + product_back(delta_key_vals, key_value_weight)
        + lax.dot_general(
            delta_maps,
            w_bc.astype(jnp.float32),
            (((1,), (1,)), ((), ())),
            precision=lax.Precision.HIGHEST,
            preferred_element_type=jnp.float32,
        )
    )
    delta_in_norm = lax.psum(delta_in_part, "tensor")
    gain_in = jnp.sum(delta_in_norm * unit_in, axis=0)
    grad_tokens = norm_back(delta_in_norm, unit_in, scale_in, norm_gains[0]) + delta_middle
    halves = lax.axis_size("tensor")
    column = jnp.arange(width, dtype=jnp.int32) // (width // halves)
    gain_share = jnp.where(
        (column == lax.axis_index("tensor"))[None, :], jnp.stack([gain_in, gain_mid]), 0.0
    )
    grad_bc, grad_conv_bc, grad_gains = (
        lax.psum_scatter(grad_bc, ("dp", "tensor"), scatter_dimension=0, tiled=True),
        lax.psum_scatter(grad_conv_bc, ("dp", "tensor"), scatter_dimension=1, tiled=True),
        lax.psum_scatter(gain_share, ("dp", "tensor"), scatter_dimension=1, tiled=True),
    )
    grad_heads, grad_conv_x, grad_ssm_gain = lax.psum(
        (grad_heads, grad_conv_x, grad_ssm_gain), "dp"
    )
    grad_zx, grad_dt, grad_out, grad_q, grad_kv, grad_o, grad_gate_up, grad_down = (
        lax.psum_scatter(grad_zx, "dp", scatter_dimension=0, tiled=True),
        lax.psum_scatter(grad_dt, "dp", scatter_dimension=0, tiled=True),
        lax.psum_scatter(grad_out, "dp", scatter_dimension=1, tiled=True),
        lax.psum_scatter(grad_q, "dp", scatter_dimension=0, tiled=True),
        lax.psum_scatter(grad_kv, "dp", scatter_dimension=0, tiled=True),
        lax.psum_scatter(grad_o, "dp", scatter_dimension=1, tiled=True),
        lax.psum_scatter(grad_gate_up, "dp", scatter_dimension=0, tiled=True),
        lax.psum_scatter(grad_down, "dp", scatter_dimension=1, tiled=True),
    )
    return (
        mixed,
        grad_tokens,
        grad_gains,
        grad_zx,
        grad_bc,
        grad_dt,
        grad_conv_x,
        grad_conv_bc,
        grad_heads,
        grad_ssm_gain,
        grad_out,
        grad_q,
        grad_kv,
        grad_o,
        grad_gate_up,
        grad_down,
    )


def solution(mesh):
    return jax.shard_map(
        on_device,
        mesh=mesh,
        in_specs=(
            P("dp", None),
            P("dp", None),
            P("dp"),
            P(),
            P(None, None, "tensor"),
            P(),
            P(None, "tensor"),
            P(None, "tensor"),
            P(),
            P(None, "tensor"),
            P("tensor"),
            P("tensor", None),
            P(None, "tensor"),
            P(None, None, "tensor"),
            P("tensor", None),
            P(None, None, "tensor"),
            P("tensor", None),
        ),
        out_specs=(
            P("dp", None),
            P("dp", None),
            P(None, ("dp", "tensor")),
            P("dp", None, "tensor"),
            P(("dp", "tensor"), None),
            P("dp", "tensor"),
            P(None, "tensor"),
            P(None, ("dp", "tensor")),
            P(None, "tensor"),
            P("tensor"),
            P("tensor", "dp"),
            P("dp", "tensor"),
            P("dp", None, "tensor"),
            P("tensor", "dp"),
            P("dp", None, "tensor"),
            P("tensor", "dp"),
        ),
        check_vma=False,
    )
```

profile of v0, /device:TPU:0, one launch (start us, length us, event | category | flops | bytes accessed | tf_op | source)
XLA Modules:
  0.0 1779.9 jit_solution(7570896897416251051)
XLA Ops:
  10.8 4.1 copy.388
  14.9 4.7 copy.256
  34.9 23.3 %fusion.251 = f32[8,128,12]{2,0,1:T(8,128)S(1)} fusion(f32[8,128,12]{2,0,1:T(8,128)S(1)} %copy.257), kind=kOutput, calls=%fused_computation.390 | output fusion | flops 1560576 | bytes 98304 | tf_op jit(solution)/shard_map/jvp(jit(cumsum))/reduce_window_sum | solution.py:107
  69.7 7.5 fusion.240
  90.7 6.4 fusion.137
  99.2 30.3 %while.63 = (s32[]{:T(128)}, f32[12,64,128]{2,1,0:T(8,128)S(1)}, f32[8,12,64,128]{3,2,1,0:T(8,128)}, f32[8,12,1,1]{1,3,2,0:T(1,128)}, f32[8,12]{1,0:T(8,128)}, /...) while((s32[]{:T(128)}, f32[12,64,128]{2,1,0:T(8,128)S(1)}, f32[8,12,64,128]{3,2,1,0:T(8,128)}, ...), condition=%wide.region_3.4_spmd.clone, body=%wide.region_2.3_spmd.clone.sunk | while | flops 393219 | bytes 1968376 | solution.py:136
  132.2 5.0 fusion.255
  138.5 13.3 bitcast_add_fusion.6
  151.9 3.8 copy.270
  155.8 6.3 multiply_reduce_fusion.13
  162.1 6.0 psum.63
  175.4 19.2 %while.62 = (s32[]{:T(128)}, bf16[2,512,1,4,64]{1,4,3,2,0:T(8,128)(2,1)}, f32[2,1,4,512]{3,2,1,0:T(4,128)}, s32[2]{0:T(128)S(1)}, s32[1024]{0:T(1024)S(1)}, /*in...) while((s32[]{:T(128)}, ...), condition=%wide.region_11.12_spmd.clone, body=%wide.region_8.11_spmd.clone.sunk | while | flops 561529344 | bytes 28425404 | solution.py:190
  196.5 4.5 fusion.237
  203.9 5.6 copy.393
  209.5 6.7 copy.272
  216.2 97.5 %all-reduce.39.cloned.1.call-done = f32[1024,1024]{1,0:T(8,128)} async-done(((f32[1024,1024]{1,0:T(8,128)}), f32[1024,1024]{1,0:T(8,128)}) %all-reduce.39.cloned.1.call-update) | async-done | bytes 4194320 | tf_op jit(solution)/shard_map/psum | solution.py:298
  317.7 4.7 fusion.210
  322.5 4.5 multiply_bitcast_fusion.1
  329.0 6.7 fusion.147
  338.2 5.3 multiply_convert_fusion.1
  344.9 4.4 fusion.257
  349.3 94.4 %all-reduce.41.cloned.1.call-done = f32[1024,1024]{1,0:T(8,128)} async-done(((f32[1024,1024]{1,0:T(8,128)}), f32[1024,1024]{1,0:T(8,128)}) %all-reduce.41.cloned.1.call-update) | async-done | bytes 4194320 | tf_op jit(solution)/shard_map/psum | solution.py:319
  443.7 5.3 multiply_reduce_fusion.1
  449.7 4.2 fusion.246
  453.9 4.3 multiply_reduce_fusion.5
  458.2 5.1 psum.67
  463.3 9.0 multiply_reduce_fusion.6
  476.2 5.4 fusion.177
  481.6 15.6 fusion.99
  497.3 4.8 fusion.133
  504.1 22.6 %while.64 = (s32[]{:T(128)}, f32[12,64,128]{2,1,0:T(8,128)S(1)}, f32[8,12]{1,0:T(8,128)S(1)}, f32[8,12,64,128]{3,2,1,0:T(8,128)}, f32[8,12,64,128]{3,2,1,0:T(8,1...) while((s32[]{:T(128)}, f32[12,64,128]{2,1,0:T(8,128)S(1)}, ...), condition=%wide.region_21.22_spmd.clone, body=%wide.region_19.21_spmd.clone.sunk | while | flops 589816 | bytes 2359724 | solution.py:136
  527.4 8.4 fusion.174
  544.1 9.0 bitcast_add_fusion.5
  556.4 5.9 copy.277
  562.4 6.8 multiply_reduce_fusion.10
  587.9 23.3 %fusion.252 = f32[8,128,12]{2,0,1:T(8,128)S(1)} fusion(f32[8,128,12]{2,0,1:T(8,128)S(1)} %copy.289), kind=kOutput, calls=%fused_computation.391 | output fusion | flops 1560576 | bytes 98304 | tf_op jit(solution)/shard_map/transpose(jvp(jit(cumsum)))/reduce_window_sum | solution.py:107
  617.8 78.7 %while.65 = (s32[]{:T(128)}, f32[1024,1,64]{0,2,1:T(8,128)S(1)}, f32[1024,1,64]{0,2,1:T(8,128)}, f32[2,512,1,4,64]{1,0,4,3,2:T(2,128)}, s32[2]{0:T(128)S(1)}, /*...) while((s32[]{:T(128)}, f32[1024,1,64]{0,2,1:T(8,128)S(1)}, ...), condition=%wide.region_30.31_spmd.clone, body=%wide.region_28.30_spmd.clone.sunk | while | flops 1375664640 | bytes 116333008 | solution.py:231
  620.1 4.6 fusion.361
  627.4 5.4 fusion.363
  638.3 10.3 dynamic_update_slice.63
  651.8 4.8 fusion.366
  659.2 4.6 fusion.361
  666.4 5.4 fusion.363
  677.4 10.3 dynamic_update_slice.63
  690.9 4.8 fusion.366
  706.7 6.5 fusion.113
  717.4 5.2 fusion.94
  727.9 12.2 fusion.90
  740.2 181.2 %all-reduce.43.cloned.1.call-done = (f32[1024,1024]{1,0:T(8,128)}, f32[1024,1024]{1,0:T(8,128)}) async-done(((f32[1024,1024]{1,0:T(8,128)}, f32[1024,1024]{1,0:T(8,128)}), (f32[1024,1024]{1,0:T(8,128)}, f32[1024,1024]{1,0:T(8,128)})) %all-reduce.43.cloned.1.call-update) | async-done | bytes 8388624 | tf_op jit(solution)/shard_map/psum | solution.py:306
  921.4 4.0 fusion.88
  926.6 8.3 fusion.108
  946.1 6.7 fusion.238
  954.4 5.6 fusion.236
  961.1 39.9 %all-reduce.32 = f32[5,256]{1,0:T(8,128)S(1)} all-reduce(f32[5,256]{1,0:T(8,128)S(1)} %pad_add_fusion.1), channel_id=6, replica_groups=mesh['dp'=16,'tensor'=2] {'dp','tensor'}, use_global_device_ids=true, to_apply=%region_51.52.clone | all-reduce | flops 1280 | bytes 10240
  1001.7 60.4 %all-reduce.33 = (f32[5,768]{1,0:T(8,128)}, f32[3,12]{1,0:T(4,128)}, f32[768]{0:T(1024)}) all-reduce(f32[5,768]{1,0:T(8,128)S(1)} %pad_add_fusion, f32[3,12]{1,0:T(4,128)S(1)} %pad_add_fusion.2, f32[768]{0:T(1024)S(1)} %copy-done.168), channel_id=1, replica_groups=mesh['dp'=16,'tensor'=2] {'dp'}, use_global_device_ids=true, to_apply=%region_45.46 | all-reduce | flops 4644 | bytes 37152 | tf_op jit(solution)/shard_map/psum | solution.py:392
  1065.8 84.4 %reduce-scatter.28.cloned.1.call-done = f32[64,2,1024]{2,0,1:T(8,128)} async-done(((f32[1024,2,1024]{2,0,1:T(8,128)}), f32[64,2,1024]{2,0,1:T(8,128)}) %reduce-scatter.28.cloned.1.call-update) | async-done | bytes 524304 | tf_op jit(solution)/shard_map/reduce_scatter | solution.py:402
  1152.4 5.7 add_convert_fusion.1
  1162.3 123.6 %reduce-scatter.32.cloned.1.call-done = f32[32,2]{1,0:T(8,128)} async-done(((f32[1024,2]{1,0:T(8,128)}), f32[32,2]{1,0:T(8,128)}) %reduce-scatter.32.cloned.1.call-update) | async-done | bytes 272
  1287.3 84.3 %reduce-scatter.16.cloned.1.call-done = f32[64,2,768]{2,0,1:T(8,128)} async-done(((f32[1024,2,768]{2,0,1:T(8,128)}), f32[64,2,768]{2,0,1:T(8,128)}) %reduce-scatter.16.cloned.1.call-update) | async-done | bytes 393232 | tf_op jit(solution)/shard_map/reduce_scatter | solution.py:396
  1373.7 58.8 %reduce-scatter.26.cloned.1.call-done = f32[256,64]{0,1:T(8,128)} async-done(((f32[256,1024]{0,1:T(8,128)}), f32[256,64]{0,1:T(8,128)}) %reduce-scatter.26.cloned.1.call-update) | async-done | bytes 65552 | tf_op jit(solution)/shard_map/reduce_scatter | solution.py:401
  1432.5 60.9 %reduce-scatter.22.cloned.1.call-done = f32[64,256]{1,0:T(8,128)} async-done(((f32[1024,256]{1,0:T(8,128)}), f32[64,256]{1,0:T(8,128)}) %reduce-scatter.22.cloned.1.call-update) | async-done | bytes 65552 | tf_op jit(solution)/shard_map/reduce_scatter | solution.py:399
  1493.4 136.6 %reduce-scatter.18.cloned.1.call-done = f32[32,256]{1,0:T(8,128)} async-done(((f32[1024,256]{1,0:T(8,128)}), f32[32,256]{1,0:T(8,128)}) %reduce-scatter.18.cloned.1.call-update) | async-done | bytes 32784 | tf_op jit(solution)/shard_map/reduce_scatter | solution.py:388
  1630.0 73.3 %reduce-scatter.30.cloned.1.call-done = f32[1024,64]{0,1:T(8,128)} async-done(((f32[1024,1024]{0,1:T(8,128)}), f32[1024,64]{0,1:T(8,128)}) %reduce-scatter.30.cloned.1.call-update) | async-done | bytes 262160 | tf_op jit(solution)/shard_map/reduce_scatter | solution.py:403
  1703.3 69.6 %reduce-scatter.20.cloned.1.call-done = f32[768,64]{0,1:T(8,128)} async-done(((f32[768,1024]{0,1:T(8,128)}), f32[768,64]{0,1:T(8,128)}) %reduce-scatter.20.cloned.1.call-update) | async-done | bytes 196624 | tf_op jit(solution)/shard_map/reduce_scatter | solution.py:398
  (659 shorter events, 256.0 us)
Async XLA Ops:
  7.2 315.3 %copy-start = (bf16[1024,1024]{1,0:T(8,128)(2,1)S(1)}, bf16[1024,1024]{1,0:T(8,128)(2,1)}, u32[]{:S(2)}) copy-start(bf16[1024,1024]{1,0:T(8,128)(2,1)} %param.41) | copy-start | bytes 6291460
  7.2 306.5 %all-reduce.39.cloned.1.call-start = ((), (), s32[]{:S(2)}) async-start(), calls=%async_computation.10 | async-start | bytes 8388608 | tf_op jit(solution)/shard_map/psum | solution.py:298
  8.7 10.9 copy-start.111
  10.8 8.9 copy-start.109
  21.9 10.7 copy-start.8
  32.1 27.6 %copy-start.62 = (s32[1024]{0:T(1024)S(1)}, s32[1024]{0:T(1024)}, u32[]{:S(2)}) copy-start(s32[1024]{0:T(1024)} %param.27) | copy-start | bytes 12292
  32.6 27.8 %copy-start.159 = (f32[12]{0:T(128)}, f32[12]{0:T(128)S(1)}, u32[]{:S(2)}) copy-start(f32[12]{0:T(128)S(1)} %get-tuple-element.686) | copy-start | bytes 148
  58.2 10.7 copy-start.145
  69.0 8.2 copy-start.113
  69.0 8.2 copy-start.115
  69.0 8.1 copy-start.117
  69.0 8.1 copy-start.119
  69.7 10.8 copy-start.121
  69.7 10.8 copy-start.123
  83.0 54.2 %copy-start.29 = (f32[1024,128]{1,0:T(8,128)}, f32[1024,128]{1,0:T(8,128)S(1)}, u32[]{:S(2)}) copy-start(f32[1024,128]{1,0:T(8,128)S(1)} %get-tuple-element.657) | copy-start | bytes 1572868
  83.0 54.2 %copy-start.31 = (f32[1024,128]{1,0:T(8,128)}, f32[1024,128]{1,0:T(8,128)S(1)}, u32[]{:S(2)}) copy-start(f32[1024,128]{1,0:T(8,128)S(1)} %get-tuple-element.656) | copy-start | bytes 1572868
  83.9 13.2 copy-start.88
  130.3 8.1 copy-start.72
  131.2 7.3 copy-start.106
  137.2 14.6 copy-start.37
  138.5 13.4 copy-start.83
  155.8 12.9 copy-start.65
  162.1 10.0 copy-start.169
  162.1 10.6 copy-start.157
  162.1 11.2 copy-start.77
  175.4 21.1 %copy-start.131 = (f32[1024]{0:T(1024)S(1)}, f32[1024]{0:T(1024)}, u32[]{:S(2)}) copy-start(f32[1024]{0:T(1024)} %get-tuple-element.677) | copy-start | bytes 12292
  175.4 21.1 %copy-start.160 = (f32[768]{0:T(1024)S(1)}, f32[768]{0:T(1024)}, u32[]{:S(2)}) copy-start(f32[768]{0:T(1024)} %param.35) | copy-start | bytes 9220
  203.9 239.9 %all-reduce.41.cloned.1.call-start = ((), (), s32[]{:S(2)}) async-start(), calls=%async_computation.11 | async-start | bytes 8388608 | tf_op jit(solution)/shard_map/psum | solution.py:319
  216.2 101.2 %copy-start.128 = (f32[1,1024]{1,0:T(1,128)S(1)}, f32[1,1024]{1,0:T(1,128)}, u32[]{:S(2)}) copy-start(f32[1,1024]{1,0:T(1,128)} %get-tuple-element.667) | copy-start | bytes 12292
  317.3 131.7 %copy-start.126 = (f32[1024]{0:T(1024)}, f32[1024]{0:T(1024)S(1)}, u32[]{:S(2)}) copy-start(f32[1024]{0:T(1024)S(1)} %add_rsqrt_fusion) | copy-start | bytes 12292
  335.7 585.7 %all-reduce.43.cloned.1.call-start = ((), (), s32[]{:S(2)}) async-start(), calls=%async_computation.22 | async-start | bytes 16777216 | tf_op jit(solution)/shard_map/psum | solution.py:306
  453.9 9.4 copy-start.136
  474.0 23.3 %copy-start.3 = (f32[96,8,8,128]{3,2,1,0:T(8,128)}, f32[96,8,8,128]{3,2,1,0:T(8,128)S(1)}, u32[]{:S(2)}) copy-start(f32[96,8,8,128]{3,2,1,0:T(8,128)S(1)} %copy.394) | copy-start | bytes 9437188
  481.6 15.7 copy-start.30
  504.1 23.2 %copy-start.71 = (f32[8,128,12]{1,2,0:T(8,128)S(1)}, f32[8,128,12]{1,2,0:T(8,128)}, u32[]{:S(2)}) copy-start(f32[8,128,12]{1,2,0:T(8,128)} %copy.265) | copy-start | bytes 147460
  527.3 8.4 copy-start.21
  527.3 8.4 copy-start.32
  540.7 21.7 %slice-start.2 = ((s8[6291456]{0:T(1024)(128)(4,1)}), s8[4194304]{0:T(1024)(128)(4,1)S(1)}, s32[]{:S(2)}) async-start(s8[6291456]{0:T(1024)(128)(4,1)} %bitcast.616), calls=%async_computation.25 | async-start | bytes 8388608
  544.1 18.2 %slice-start.3 = ((s8[6291456]{0:T(1024)(128)(4,1)}), s8[2097152]{0:T(1024)(128)(4,1)S(1)}, s32[]{:S(2)}) async-start(s8[6291456]{0:T(1024)(128)(4,1)} %bitcast.616), calls=%async_computation.26 | async-start | bytes 4194304
  544.1 18.2 %copy-start.24 = (f32[1023,768]{0,1:T(8,128)S(1)}, f32[1023,768]{0,1:T(8,128)}, u32[]{:S(2)}) copy-start(f32[1023,768]{0,1:T(8,128)} %slice_bitcast_fusion.5) | copy-start | bytes 9427972
  544.1 18.2 %copy-start.26 = (f32[1024,768]{0,1:T(8,128)S(1)}, f32[1024,768]{0,1:T(8,128)}, u32[]{:S(2)}) copy-start(f32[1024,768]{0,1:T(8,128)} %copy-done.25) | copy-start | bytes 9437188
  553.2 9.2 copy-start.23
  562.4 6.8 copy-start.120
  562.4 6.8 copy-start.154
  569.2 10.2 copy-start.11
  699.9 6.8 copy-start.50
  706.7 6.6 copy-start.92
  722.7 340.1 %reduce-scatter.34.cloned.1.call-start = ((), (), s32[]{:S(2)}) async-start(), calls=%async_computation.21 | async-start | bytes 557056
  725.8 338.4 %reduce-scatter.24.cloned.1.call-start = ((), (), s32[]{:S(2)}) async-start(), calls=%async_computation.16 | async-start | bytes 1114112 | tf_op jit(solution)/shard_map/reduce_scatter | solution.py:400
  727.6 422.5 %reduce-scatter.28.cloned.1.call-start = ((), (), s32[]{:S(2)}) async-start(), calls=%async_computation.18 | async-start | bytes 8912896 | tf_op jit(solution)/shard_map/reduce_scatter | solution.py:402
  740.1 181.3 %copy-start.110 = (f32[1024]{0:T(1024)S(1)}, f32[1024]{0:T(1024)}, u32[]{:S(2)}) copy-start(f32[1024]{0:T(1024)} %copy-done.109) | copy-start | bytes 12292
  740.1 181.3 %copy-start.112 = (f32[1,1024]{1,0:T(1,128)S(1)}, f32[1,1024]{1,0:T(1,128)}, u32[]{:S(2)}) copy-start(f32[1,1024]{1,0:T(1,128)} %copy-done.111) | copy-start | bytes 12292
  740.2 545.8 %reduce-scatter.32.cloned.1.call-start = ((), (), s32[]{:S(2)}) async-start(), calls=%async_computation.20 | async-start | bytes 540672
  926.5 445.1 %reduce-scatter.16.cloned.1.call-start = ((), (), s32[]{:S(2)}) async-start(), calls=%async_computation.12 | async-start | bytes 6684672 | tf_op jit(solution)/shard_map/reduce_scatter | solution.py:396
  934.9 497.6 %reduce-scatter.26.cloned.1.call-start = ((), (), s32[]{:S(2)}) async-start(), calls=%async_computation.17 | async-start | bytes 1114112 | tf_op jit(solution)/shard_map/reduce_scatter | solution.py:401
  939.5 553.9 %reduce-scatter.22.cloned.1.call-start = ((), (), s32[]{:S(2)}) async-start(), calls=%async_computation.15 | async-start | bytes 1114112 | tf_op jit(solution)/shard_map/reduce_scatter | solution.py:399
  942.4 687.6 %reduce-scatter.18.cloned.1.call-start = ((), (), s32[]{:S(2)}) async-start(), calls=%async_computation.13 | async-start | bytes 1081344 | tf_op jit(solution)/shard_map/reduce_scatter | solution.py:388
  946.1 757.3 %reduce-scatter.30.cloned.1.call-start = ((), (), s32[]{:S(2)}) async-start(), calls=%async_computation.19 | async-start | bytes 4456448 | tf_op jit(solution)/shard_map/reduce_scatter | solution.py:403
  952.8 820.1 %reduce-scatter.20.cloned.1.call-start = ((), (), s32[]{:S(2)}) async-start(), calls=%async_computation.14 | async-start | bytes 3342336 | tf_op jit(solution)/shard_map/reduce_scatter | solution.py:398
  960.1 40.8 %copy-start.175 = (f32[12]{0:T(128)S(1)}, f32[12]{0:T(128)}, u32[]{:S(2)}) copy-start(f32[12]{0:T(128)} %get-tuple-element.662) | copy-start | bytes 148
  960.1 41.5 %copy-start.172 = (f32[12]{0:T(128)S(1)}, f32[12]{0:T(128)}, u32[]{:S(2)}) copy-start(f32[12]{0:T(128)} %get-tuple-element.630) | copy-start | bytes 148
  960.1 41.5 %copy-start.168 = (f32[768]{0:T(1024)S(1)}, f32[768]{0:T(1024)}, u32[]{:S(2)}) copy-start(f32[768]{0:T(1024)} %get-tuple-element.539) | copy-start | bytes 9220
  1152.4 7.3 copy-start.35
  1159.7 613.3 %copy-start.1 = (bf16[1024,1024]{1,0:T(8,128)(2,1)S(1)}, bf16[1024,1024]{1,0:T(8,128)(2,1)}, u32[]{:S(2)}) copy-start(bf16[1024,1024]{1,0:T(8,128)(2,1)} %param.41) | copy-start | bytes 6291460
  (138 other events, 434.2 us)
Sparse Core Ops, SparseCore 0:
  204.0 109.6 all-reduce.38
  335.8 107.8 all-reduce.40
  722.8 198.5 all-reduce.42
  925.4 56.1 reduce-scatter.33
  986.1 56.5 reduce-scatter.23
  1046.6 103.5 reduce-scatter.27
  1152.4 133.4 reduce-scatter.31
  1290.4 81.1 reduce-scatter.15
  1375.8 56.6 reduce-scatter.25
  1436.9 56.3 reduce-scatter.21
  1496.2 133.7 reduce-scatter.17
  1634.8 68.5 reduce-scatter.29
  1707.7 65.1 reduce-scatter.19
where the time goes:
time: 1790 us; the launch traced here: 1780 us
  waiting for transfers between devices  1060 us (59%)
  matrix products  231 us (13%)
  other arithmetic  200 us (11%)
  local copies, waits for them, and re-layouts  147 us (8%)
  blocking collectives  111 us (6%)
    psum x1, waiting for transfers between devices, on_device(): middle_out = middle + lax.psum(product(activation, w_down), 'tensor')  181 us
    reduce_scatter x1, waiting for transfers between devices, on_device(): lax.psum_scatter(grad_bc, ('dp', 'tensor'), scatter_dimension=0, tiled=True)  137 us
    unnamed x15, waiting for transfers between devices  124 us
    psum x1, waiting for transfers between devices, on_device(): middle = resid + lax.psum(partial_mix, 'tensor')  97.5 us
    psum x1, waiting for transfers between devices, on_device(): lax.psum(product_back(delta_gate_up, gate_up_weight), 'tensor')  94.4 us
    reduce_scatter x1, waiting for transfers between devices, on_device(): lax.psum_scatter(grad_gate_up, 'dp', scatter_dimension=0, tiled=True)  84.4 us
    reduce_scatter x1, waiting for transfers between devices, on_device(): lax.psum_scatter(grad_zx, 'dp', scatter_dimension=0, tiled=True)  84.3 us
    reduce_scatter x1, waiting for transfers between devices, on_device(): lax.psum_scatter(grad_down, 'dp', scatter_dimension=1, tiled=True)  73.3 us
  transfers between devices with their start and end apart: 13, of which 11 were waited for; matrix products, arithmetic and copies ran while one was open for 5% of the time, Pallas kernels for 0%

commit v1 on v0

v1 whole, which is shorter than its diff:
```python
import math

import jax
import jax.numpy as jnp
from jax import lax
from jax.sharding import PartitionSpec as P

SSM_HEAD_DIM = 64
ATT_HEAD_DIM = 64
SPAN = 128
INNER = 1536
ATT_BLOCK = 256
PIECES = 2
PRECISE = lax.Precision.HIGH


EPS = 1e-05
ROPE_BASE = 100000000000.0


def product(left, right):
    return jnp.dot(left, right, preferred_element_type=jnp.float32)


def product_back(left, right):
    return lax.dot_general(
        left, right, (((1,), (1,)), ((), ())), preferred_element_type=jnp.float32
    )


def weight_product(left, right):
    return lax.dot_general(
        left, right, (((0,), (0,)), ((), ())), preferred_element_type=jnp.float32
    )


def norm_scale(values):
    return lax.rsqrt(jnp.mean(values * values, axis=-1, keepdims=True) + EPS)


def norm_back(grad_normed, unit, scale, gain):
    grad_unit = grad_normed * gain[None, :]
    return scale * (grad_unit - unit * jnp.mean(grad_unit * unit, axis=-1, keepdims=True))


def token_places(segments):
    count = segments.shape[0]
    index = jnp.arange(count, dtype=jnp.int32)
    starts = jnp.concatenate([jnp.ones((1,), dtype=bool), segments[1:] != segments[:-1]])
    first = lax.cummax(jnp.where(starts, index, 0), axis=0)
    return (index - first).astype(jnp.float32)


def rotary_tables(places, head_dim):
    half = head_dim // 2
    freqs = jnp.exp(jnp.arange(half, dtype=jnp.float32) * (-2.0 * math.log(ROPE_BASE) / head_dim))
    angle = places[:, None] * freqs[None, :]
    return (jnp.cos(angle), jnp.sin(angle))


def rotate(values, cosines, sines):
    half = values.shape[-1] // 2
    first = values[..., :half]
    second = values[..., half:]
    cosines = cosines[:, None, :]
    sines = sines[:, None, :]
    return jnp.concatenate(
        [first * cosines - second * sines, second * cosines + first * sines], axis=-1
    )


def rotate_back(grads, cosines, sines):
    half = grads.shape[-1] // 2
    first = grads[..., :half]
    second = grads[..., half:]
    cosines = cosines[:, None, :]
    sines = sines[:, None, :]
    return jnp.concatenate(
        [first * cosines + second * sines, second * cosines - first * sines], axis=-1
    )


def causal_filter(values, taps, segments):
    total = values.shape[0]
    width = taps.shape[0] - 1
    result = taps[width][None, :] + taps[0][None, :] * values
    for offset in range(1, width):
        earlier = jnp.concatenate(
            [jnp.zeros((offset, values.shape[1]), values.dtype), values[: total - offset]]
        )
        earlier_seg = jnp.concatenate(
            [jnp.full((offset,), -2, jnp.int32), segments[: total - offset]]
        )
        result = (
            result
            + jnp.where((earlier_seg == segments)[:, None], earlier, 0.0) * taps[offset][None, :]
        )
    return result


def state_space(inputs, steps, rates, b_mat, c_mat, segments):
    total, heads, head_dim = inputs.shape
    nstate = b_mat.shape[1]
    count = total // SPAN
    step_blocks = steps.reshape(count, SPAN, heads).transpose(0, 2, 1)
    x_blocks = inputs.reshape(count, SPAN, heads, head_dim).transpose(0, 2, 1, 3)
    x_blocks = x_blocks * step_blocks[..., None]
    b_blocks = b_mat.reshape(count, SPAN, nstate)
    c_blocks = c_mat.reshape(count, SPAN, nstate)
    seg_blocks = segments.reshape(count, SPAN)
    lower = jnp.tril(jnp.ones((SPAN, SPAN), jnp.float32))
    decay_sum = jnp.einsum(
        "chj,ij->chi", -step_blocks * rates[None, :, None], lower, precision=lax.Precision.HIGHEST
    )
    inside = (seg_blocks[:, :, None] == seg_blocks[:, None, :]) & (lower > 0)[None]
    gap = decay_sum[:, :, :, None] - decay_sum[:, :, None, :]
    weights = jnp.exp(jnp.where(inside[:, None], gap, -1e30))
    intersection = jnp.einsum("cin,cjn->cij", c_blocks, b_blocks, precision=PRECISE)
    weights = weights * intersection[:, None]
    within = jnp.einsum("chij,chjp->chip", weights, x_blocks, precision=PRECISE)
    last_seg = seg_blocks[:, -1]
    final = decay_sum[:, :, -1]
    tail = (seg_blocks == last_seg[:, None]).astype(jnp.float32)[:, None, :] * jnp.exp(
        final[:, :, None] - decay_sum
    )
    block_state = jnp.einsum(
        "chjp,cjn->chpn", x_blocks * tail[..., None], b_blocks, precision=PRECISE
    )
    carry_on = (last_seg[1:] == last_seg[:-1]).astype(jnp.float32)
    factor = jnp.exp(final[1:]) * carry_on[:, None]
    state = jnp.zeros((heads, head_dim, nstate), jnp.float32)
    entering = [state]
    for number in range(count - 1):
        if number == 0:
            state = block_state[0]
        else:
            state = factor[number - 1][:, None, None] * state + block_state[number]
        entering.append(state)
    entering = jnp.stack(entering)
    previous = jnp.concatenate([jnp.full((1,), -3, jnp.int32), last_seg[:-1]])
    head_weight = (seg_blocks == previous[:, None]).astype(jnp.float32)[:, None, :] * jnp.exp(
        decay_sum
    )
    carried = (
        jnp.einsum("cin,chpn->chip", c_blocks, entering, precision=PRECISE)
        * head_weight[..., None]
    )
    return (within + carried).transpose(0, 2, 1, 3).reshape(total, heads, head_dim)


def mixer_core(gate_and_x, step_raw, state_maps, conv_x, conv_bc, head_params, segments):
    total = gate_and_x.shape[0]
    heads = step_raw.shape[1]
    z_part = gate_and_x[:, 0]
    x_part = jax.nn.silu(causal_filter(gate_and_x[:, 1], conv_x, segments))
    maps = jax.nn.silu(causal_filter(state_maps, conv_bc, segments))
    nstate = state_maps.shape[1] // 2
    x_heads = x_part.reshape(total, heads, SSM_HEAD_DIM)
    rates = jnp.exp(head_params[0])
    steps = jax.nn.softplus(step_raw + head_params[1][None, :])
    output = state_space(x_heads, steps, rates, maps[:, :nstate], maps[:, nstate:], segments)
    output = output + head_params[2][None, :, None] * x_heads
    return output.reshape(total, heads * SSM_HEAD_DIM) * jax.nn.silu(z_part)


def block_scores(queries, keys, segments, start, stop, scale):
    part = queries[start:stop]
    scores = jnp.einsum(
        "ikgd,jkd->kgij", part, keys[:stop], preferred_element_type=jnp.float32
    ) * scale
    rows_here = jnp.arange(start, stop, dtype=jnp.int32)
    index = jnp.arange(stop, dtype=jnp.int32)
    allowed = (segments[start:stop, None] == segments[None, :stop]) & (
        rows_here[:, None] >= index[None, :]
    )
    return jnp.where(allowed[None, None], scores, -1e30)


def attend(queries, keys, values, segments):
    total = queries.shape[0]
    block = min(ATT_BLOCK, total)
    scale = queries.shape[-1] ** (-0.5)
    outputs, log_sums = [], []
    for start in range(0, total, block):
        stop = start + block
        scores = block_scores(queries, keys, segments, start, stop, scale)
        log_sum = jax.nn.logsumexp(scores, axis=-1)
        probs = jnp.exp(scores - log_sum[..., None]).astype(jnp.bfloat16)
        outputs.append(
            jnp.einsum("kgij,jkd->ikgd", probs, values[:stop], preferred_element_type=jnp.float32)
        )
        log_sums.append(log_sum)
    return (jnp.concatenate(outputs), log_sums)


def attend_back(queries, keys, values, segments, log_sums, grad_out):
    total = queries.shape[0]
    block = min(ATT_BLOCK, total)
    scale = queries.shape[-1] ** (-0.5)
    grad_parts = []
    grad_keys = jnp.zeros(keys.shape, jnp.float32)
    grad_values = jnp.zeros(keys.shape, jnp.float32)
    for number, start in enumerate(range(0, total, block)):
        stop = start + block
        part = queries[start:stop]
        part_grad = grad_out[start:stop]
        scores = block_scores(queries, keys, segments, start, stop, scale)
        probs = jnp.exp(scores - log_sums[number][..., None])
        grad_probs = jnp.einsum(
            "ikgd,jkd->kgij", part_grad, values[:stop], preferred_element_type=jnp.float32
        )
        grad_scores = (
            probs * (grad_probs - jnp.sum(probs * grad_probs, axis=-1, keepdims=True))
        ).astype(jnp.bfloat16)
        grad_parts.append(
            jnp.einsum(
                "kgij,jkd->ikgd", grad_scores, keys[:stop], preferred_element_type=jnp.float32
            )
            * scale
        )
        key_part = (
            jnp.einsum("kgij,ikgd->jkd", grad_scores, part, preferred_element_type=jnp.float32)
            * scale
        )
        value_part = jnp.einsum(
            "kgij,ikgd->jkd",
            probs.astype(jnp.bfloat16),
            part_grad,
            preferred_element_type=jnp.float32,
        )
        grad_keys = grad_keys.at[:stop].add(key_part)
        grad_values = grad_values.at[:stop].add(value_part)
    return (jnp.concatenate(grad_parts), grad_keys, grad_values)


def other_half(values):
    halves = lax.axis_size("tensor")
    return lax.ppermute(values, "tensor", [(i, (i + 1) % halves) for i in range(halves)])


def on_device(
    tokens,
    out_grad,
    segment_ids,
    norm_gains,
    w_zx,
    w_bc,
    w_dt,
    conv_x,
    conv_bc,
    head_params,
    ssm_gain,
    w_out,
    w_q,
    w_kv,
    w_o,
    w_gate_up,
    w_down,
):
    total, width = tokens.shape
    inner_local = w_zx.shape[2]
    heads_local = w_dt.shape[1]
    hidden_local = w_gate_up.shape[2]
    nmaps = w_bc.shape[1]
    key_heads = w_kv.shape[2] // ATT_HEAD_DIM
    query_heads = w_q.shape[1] // ATT_HEAD_DIM
    group = query_heads // key_heads
    key_width = key_heads * ATT_HEAD_DIM
    query_width = query_heads * ATT_HEAD_DIM
    gate_up_weight = w_gate_up.reshape(width, 2 * hidden_local)
    step_pad = -heads_local % 128
    in_weight = jnp.concatenate(
        [
            w_zx.reshape(width, 2 * inner_local),
            w_q,
            w_kv.reshape(width, 2 * key_width),
            w_bc,
            jnp.pad(w_dt, ((0, 0), (0, step_pad))),
        ],
        axis=1,
    )
    at_q = 2 * inner_local
    at_kv = at_q + query_width
    at_bc = at_kv + 2 * key_width
    at_dt = at_bc + nmaps
    resid = tokens.astype(jnp.float32)
    live = (segment_ids >= 0).astype(jnp.float32)[:, None]
    cotangent = (out_grad.astype(jnp.float32) * live).astype(jnp.bfloat16)
    scale_in = norm_scale(resid)
    unit_in = resid * scale_in
    normed_in = (unit_in * norm_gains[0][None, :]).astype(jnp.bfloat16)
    projected = product(normed_in, in_weight)
    gate_and_x = projected[:, :at_q].reshape(total, 2, inner_local)
    state_maps = projected[:, at_bc:at_dt]
    step_raw = projected[:, at_dt : at_dt + heads_local]

    def local_mixer(first, second, third, fourth, fifth, sixth):
        return mixer_core(first, second, third, fourth, fifth, sixth, segment_ids)

    gated, mixer_pullback = jax.vjp(
        local_mixer, gate_and_x, step_raw, state_maps, conv_x, conv_bc, head_params
    )
    squares = lax.psum(jnp.sum(gated * gated, axis=1), "tensor")
    scale_ssm = lax.rsqrt(squares[:, None] / INNER + EPS)
    unit_ssm = gated * scale_ssm
    mixed_ssm = (unit_ssm * ssm_gain[None, :]).astype(jnp.bfloat16)
    cosines, sines = rotary_tables(token_places(segment_ids), ATT_HEAD_DIM)
    queries = projected[:, at_q:at_kv].reshape(total, query_heads, ATT_HEAD_DIM)
    key_vals = projected[:, at_kv:at_bc].reshape(total, 2, key_heads, ATT_HEAD_DIM)
    queries = (
        rotate(queries, cosines, sines)
        .astype(jnp.bfloat16)
        .reshape(total, key_heads, group, ATT_HEAD_DIM)
    )
    keys = rotate(key_vals[:, 0], cosines, sines).astype(jnp.bfloat16)
    values = key_vals[:, 1].astype(jnp.bfloat16)
    attended, log_sums = attend(queries, keys, values, segment_ids)
    attended = attended.astype(jnp.bfloat16).reshape(total, query_width)
    mixed_in = jnp.concatenate([mixed_ssm, attended], axis=1)
    mix_weight = jnp.concatenate([w_out, w_o], axis=0)
    piece = total // PIECES
    middle, middle_down, unit_mid, scale_mid = [], [], [], []
    normed_mid, activation, delta_gate_up, delta_partial = [], [], [], []
    mix_parts = [
        product(mixed_in[n * piece : (n + 1) * piece], mix_weight) for n in range(PIECES)
    ]
    mix_sent = [other_half(part) for part in mix_parts]
    for n in range(PIECES):
        rows = slice(n * piece, (n + 1) * piece)
        middle_n = resid[rows] + (mix_parts[n] + mix_sent[n])
        scale_n = norm_scale(middle_n)
        unit_n = middle_n * scale_n
        normed_n = (unit_n * norm_gains[1][None, :]).astype(jnp.bfloat16)
        gate_up = product(normed_n, gate_up_weight)
        gate = gate_up[:, :hidden_local]
        upper = gate_up[:, hidden_local:]
        delta_act = product_back(cotangent[rows], w_down)
        sigma = jax.nn.sigmoid(gate)
        activation_n = (gate * sigma * upper).astype(jnp.bfloat16)
        delta_gate = delta_act * upper * sigma * (1.0 + gate * (1.0 - sigma))
        delta_upper = delta_act * (gate * sigma)
        delta_n = jnp.concatenate([delta_gate, delta_upper], axis=1).astype(jnp.bfloat16)
        partial_n = product_back(delta_n, gate_up_weight)
        middle.append(middle_n)
        scale_mid.append(scale_n)
        unit_mid.append(unit_n)
        normed_mid.append(normed_n)
        activation.append(activation_n)
        delta_gate_up.append(delta_n)
        delta_partial.append(partial_n)
    delta_sent = [other_half(part) for part in delta_partial]
    activation = jnp.concatenate(activation)
    delta_gate_up = jnp.concatenate(delta_gate_up)
    normed_mid = jnp.concatenate(normed_mid)
    feed_grads = jnp.concatenate(
        [weight_product(normed_mid, delta_gate_up), weight_product(cotangent, activation)], axis=1
    )
    gain_mid = sum(jnp.sum(part * unit, axis=0) for part, unit in zip(delta_partial, unit_mid))
    delta_middle = jnp.concatenate(
        [
            norm_back(part + sent, unit, scale, norm_gains[1])
            for part, sent, unit, scale in zip(delta_partial, delta_sent, unit_mid, scale_mid)
        ]
    ) + cotangent.astype(jnp.float32)
    delta_middle, feed_grads = lax.optimization_barrier((delta_middle, feed_grads))
    feed_grads = lax.psum_scatter(feed_grads, "dp", scatter_dimension=0, tiled=True)
    delta_mix = delta_middle.astype(jnp.bfloat16)
    out_part = product(activation, w_down)
    out_sent = other_half(out_part)
    mix_grads = weight_product(delta_mix, mixed_in)
    delta_ssm = product_back(delta_mix, w_out)
    delta_attended = (
        product_back(delta_mix, w_o)
        .astype(jnp.bfloat16)
        .reshape(total, key_heads, group, ATT_HEAD_DIM)
    )
    grad_ssm_gain = jnp.sum(delta_ssm * unit_ssm, axis=0)
    delta_unit = delta_ssm * ssm_gain[None, :]
    across = lax.psum(jnp.sum(delta_unit * gated, axis=1), "tensor")
    delta_gated = scale_ssm * delta_unit - gated * scale_ssm**3 * (across[:, None] / INNER)
    delta_gx, delta_step, delta_maps, grad_conv_x, grad_conv_bc, grad_heads = mixer_pullback(
        delta_gated
    )
    delta_queries, delta_keys, delta_values = attend_back(
        queries, keys, values, segment_ids, log_sums, delta_attended
    )
    delta_queries = rotate_back(
        delta_queries.reshape(total, query_heads, ATT_HEAD_DIM), cosines, sines
    ).reshape(total, query_width)
    delta_keys = rotate_back(delta_keys, cosines, sines).reshape(total, key_width)
    delta_in = jnp.concatenate(
        [
            delta_gx.reshape(total, 2 * inner_local).astype(jnp.bfloat16),
            delta_queries.astype(jnp.bfloat16),
            delta_keys.astype(jnp.bfloat16),
            delta_values.reshape(total, key_width).astype(jnp.bfloat16),
            delta_maps.astype(jnp.bfloat16),
            jnp.pad(delta_step, ((0, 0), (0, step_pad))).astype(jnp.bfloat16),
        ],
        axis=1,
    )
    in_part = product_back(delta_in, in_weight)
    in_sent = other_half(in_part)
    in_grads = weight_product(normed_in, delta_in)
    mix_grads, feed_grads = lax.optimization_barrier((mix_grads, feed_grads))
    mix_grads = lax.psum_scatter(mix_grads, "dp", scatter_dimension=0, tiled=True)
    in_grads, mix_grads = lax.optimization_barrier((in_grads, mix_grads))
    in_grads = lax.psum_scatter(in_grads, "dp", scatter_dimension=0, tiled=True)
    gain_in = jnp.sum(in_part * unit_in, axis=0)
    inner_n = conv_x.shape[0] * inner_local
    maps_n = conv_bc.shape[0] * nmaps
    small = jnp.concatenate(
        [
            grad_conv_bc.reshape(maps_n),
            gain_in,
            gain_mid,
            grad_conv_x.reshape(inner_n),
            grad_ssm_gain,
            grad_heads.reshape(-1),
        ]
    )
    small = lax.psum(small, "dp")
    at_conv = maps_n + 2 * width
    at_gain = at_conv + inner_n
    at_heads = at_gain + inner_local
    grad_conv_x = small[at_conv:at_gain].reshape(conv_x.shape)
    grad_ssm_gain = small[at_gain:at_heads]
    grad_heads = small[at_heads:].reshape(head_params.shape)
    halves = lax.axis_size("tensor")
    where_tensor = lax.axis_index("tensor")
    bc_rows = in_grads[:, at_bc:at_dt]
    shared, bc_rows = lax.psum((small[:at_conv], bc_rows), "tensor")
    bc_size = bc_rows.shape[0] // halves
    grad_bc = lax.dynamic_slice_in_dim(bc_rows, where_tensor * bc_size, bc_size, 0)
    place = lax.axis_index("dp") * halves + where_tensor
    count = lax.axis_size("dp") * halves
    conv_cols = nmaps // count
    gain_cols = width // count
    grad_conv_bc = lax.dynamic_slice_in_dim(
        shared[:maps_n].reshape(conv_bc.shape), place * conv_cols, conv_cols, 1
    )
    grad_gains = lax.dynamic_slice_in_dim(
        shared[maps_n:].reshape(2, width), place * gain_cols, gain_cols, 1
    )
    grad_tokens = (
        norm_back(in_part + in_sent, unit_in, scale_in, norm_gains[0]) + delta_middle
    )
    mixed = (jnp.concatenate(middle) + (out_part + out_sent)).astype(jnp.bfloat16)
    mine = in_grads.shape[0]
    grad_zx = in_grads[:, :at_q].reshape(mine, 2, inner_local)
    grad_q = in_grads[:, at_q:at_kv]
    grad_kv = in_grads[:, at_kv:at_bc].reshape(mine, 2, key_width)
    grad_dt = in_grads[:, at_dt : at_dt + heads_local]
    grad_gate_up = feed_grads[:, : 2 * hidden_local].reshape(mine, 2, hidden_local)
    grad_down = feed_grads[:, 2 * hidden_local :].T
    grad_out = mix_grads[:, :inner_local].T
    grad_o = mix_grads[:, inner_local:].T
    return (
        mixed,
        grad_tokens,
        grad_gains,
        grad_zx,
        grad_bc,
        grad_dt,
        grad_conv_x,
        grad_conv_bc,
        grad_heads,
        grad_ssm_gain,
        grad_out,
        grad_q,
        grad_kv,
        grad_o,
        grad_gate_up,
        grad_down,
    )


def solution(mesh):
    return jax.shard_map(
        on_device,
        mesh=mesh,
        in_specs=(
            P("dp", None),
            P("dp", None),
            P("dp"),
            P(),
            P(None, None, "tensor"),
            P(),
            P(None, "tensor"),
            P(None, "tensor"),
            P(),
            P(None, "tensor"),
            P("tensor"),
            P("tensor", None),
            P(None, "tensor"),
            P(None, None, "tensor"),
            P("tensor", None),
            P(None, None, "tensor"),
            P("tensor", None),
        ),
        out_specs=(
            P("dp", None),
            P("dp", None),
            P(None, ("dp", "tensor")),
            P("dp", None, "tensor"),
            P(("dp", "tensor"), None),
            P("dp", "tensor"),
            P(None, "tensor"),
            P(None, ("dp", "tensor")),
            P(None, "tensor"),
            P("tensor"),
            P("tensor", "dp"),
            P("dp", "tensor"),
            P("dp", None, "tensor"),
            P("tensor", "dp"),
            P("dp", None, "tensor"),
            P("tensor", "dp"),
        ),
        check_vma=False,
    )
```

time: 1790 us -> 883 us (0.49)
  waiting for transfers between devices: 1060 us -> 386 us
  matrix products: 231 us -> 136 us
  other arithmetic: 200 us -> 128 us
  blocking collectives: 111 us -> 77.5 us
  local copies, waits for them, and re-layouts: 147 us -> 123 us
    reduce_scatter x8 -> x3, waiting for transfers between devices: 568 us -> 58.3 us  [the longest x1 48 us: on_device(): lax.psum_scatter(mix_grads, 'dp', scatter_dimension=0, tiled=True)]
    psum x3 -> x1, waiting for transfers between devices: 373 us -> 10.5 us  [on_device(): shared, bc_rows = lax.psum((small[:at_conv], bc_rows), 'tensor')]
    ppermute x0 -> x6, waiting for transfers between devices: none -> 317 us  [other_half(): lax.ppermute(values, 'tensor', [(i, (i + 1) % halves) for i in range(halv...]
    unnamed x15 -> x4, waiting for transfers between devices: 124 us -> 0.07 us
    dot_general x28 -> x38, matrix products: 132 us -> 62.4 us  [the longest x3 21.7 us: state_space(): within = jnp.einsum('chij,chjp->chip', weights, x_blocks, precision=PRECISE)]
    another operation x11 -> x12, other arithmetic: 53.3 us -> 7.39 us  [the longest x2 46.6 us: state_space(): decay_sum = jnp.cumsum(-step_blocks * rates[None, None, :], axis=1)]
    unnamed x1 -> x0, blocking collectives: 39.9 us -> none
    dynamic_update_slice x20 -> x0, local copies, waits for them, and re-layouts: 31.9 us -> none  [the longest x4 21.8 us: attend(): lax.map(one_block, jnp.arange(total // block, dtype=jnp.int32))]
  transfers between devices with their start and end apart: 13 -> 10, of which waited for: 11 -> 9; matrix products, arithmetic and copies ran while one was open for 5% -> 23% of each run, Pallas kernels for 0% -> 0%
where the time goes in v1:
time: 883 us; the launch traced here: 875 us
  waiting for transfers between devices  386 us (44%)
  matrix products  136 us (15%)
  other arithmetic  128 us (14%)
  local copies, waits for them, and re-layouts  123 us (14%)
  blocking collectives  77.5 us (9%)
  between operations  17.6 us (2%)
    ppermute x6, waiting for transfers between devices, other_half(): lax.ppermute(values, 'tensor', [(i, (i + 1) % halves) for i in range(halv...  317 us
    psum x1, blocking collectives, on_device(): small = lax.psum(small, 'dp')  57.7 us
    reduce_scatter x1, waiting for transfers between devices, on_device(): lax.psum_scatter(mix_grads, 'dp', scatter_dimension=0, tiled=True)  48 us
    unnamed x563, local copies, waits for them, and re-layouts  47.6 us
    dot_general x7, matrix products, product_back(): lax.dot_general(left, right, (((1,), (1,)), ((), ())), preferred_element_...  27.6 us
    dot_general x4, matrix products, weight_product(): lax.dot_general(left, right, (((0,), (0,)), ((), ())), preferred_element_...  24.1 us
    dot_general x3, matrix products, state_space(): within = jnp.einsum('chij,chjp->chip', weights, x_blocks, precision=PRECISE)  21.7 us
    dot_general x6, matrix products, product(): return jnp.dot(left, right, preferred_element_type=jnp.float32)  21.7 us
  transfers between devices with their start and end apart: 10, of which 9 were waited for; matrix products, arithmetic and copies ran while one was open for 23% of the time, Pallas kernels for 0%

profile of v1, /device:TPU:0, one launch (start us, length us, event | category | flops | bytes accessed | tf_op | source)
XLA Modules:
  0.0 874.8 jit_solution(3115548266380907230)
XLA Ops:
  22.3 2.5 copy.272
  28.2 5.1 fusion.151
  33.4 3.6 copy-done.41
  42.3 2.6 slice.704
  44.9 2.3 slice.703
  47.3 5.8 slice.708
  53.1 7.1 copy.269
  60.2 4.1 slice_bitcast_fusion.1
  72.0 2.7 constant_dynamic-update-slice_fusion.10
  78.8 3.6 fusion.145
  100.7 4.0 fusion.262
  113.0 7.0 fusion.40
  120.1 2.2 copy.212
  122.3 4.4 multiply_reduce_fusion.11
  126.7 6.6 psum.35
  136.5 2.2 multiply_convert_fusion.2
  138.7 6.7 maximum_maximum_fusion
  146.8 2.1 collective-permute-start
  152.4 3.5 copy.275
  156.3 39.2 %collective-permute-done = f32[512,1024]{1,0:T(8,128)S(1)} collective-permute-done((f32[512,1024]{1,0:T(8,128)S(1)}, f32[512,1024]{1,0:T(8,128)S(1)}, u32[]{:S(2)}, u32[]{:S(2)}) %collective-permute-start) | collective-permute-done | bytes 2097184 | tf_op jit(solution)/shard_map/ppermute | solution.py:238
  196.8 41.7 %collective-permute-done.1 = f32[512,1024]{1,0:T(8,128)} collective-permute-done((f32[512,1024]{1,0:T(8,128)S(1)}, f32[512,1024]{1,0:T(8,128)}, u32[]{:S(2)}, u32[]{:S(2)}) %collective-permute-start.1) | collective-permute-done | bytes 2097184 | tf_op jit(solution)/shard_map/ppermute | solution.py:238
  238.4 3.1 multiply_reduce_fusion.17
  241.9 5.8 fusion.284
  249.8 2.4 fusion.67
  254.0 43.8 %collective-permute-done.3 = f32[512,1024]{1,0:T(8,128)S(1)} collective-permute-done((f32[512,1024]{1,0:T(8,128)S(1)}, f32[512,1024]{1,0:T(8,128)S(1)}, u32[]{:S(2)}, u32[]{:S(2)}) %collective-permute-start.3) | collective-permute-done | bytes 2097184 | tf_op jit(solution)/shard_map/ppermute | solution.py:238
  299.4 2.5 fusion.285
  304.0 3.7 fusion.71
  309.2 2.5 fusion.96
  312.3 4.7 fusion.6
  317.0 5.1 pad_maximum_fusion
  322.1 30.6 %collective-permute-done.4 = f32[512,1024]{1,0:T(8,128)} collective-permute-done((f32[512,1024]{1,0:T(8,128)}, f32[512,1024]{1,0:T(8,128)}, u32[]{:S(2)}, u32[]{:S(2)}) %collective-permute-start.4) | collective-permute-done | bytes 2097184 | tf_op jit(solution)/shard_map/ppermute | solution.py:238
  352.7 4.1 multiply_reduce_fusion.12
  356.9 3.5 subtract_multiply_fusion.3
  360.4 2.5 maximum_add_fusion.1
  368.2 3.7 convolution_convert_fusion
  377.3 4.4 multiply_reduce_fusion.5
  381.7 4.9 psum.36
  386.6 9.5 %multiply_reduce_fusion.4 = (f32[768]{0:T(1024)}, f32[1024,768]{0,1:T(8,128)S(1)}, f32[1024,1,768]{0,2,1:T(8,128)}) fusion(f32[1024,768]{0,1:T(8,128)} %copy-done.18, f32[1024,2,768]{0,2,1:T(8,128)} %bitcast.653, f32[1024]{0:T(1024)S(1)} %broadcast_multiply_fusion, f32[1024,768]{0,1:T(8,128)} %get-tuple-element.275, f32[1024]{0:T(1024)S(1)} %copy-done.199, ...), kind=kLoop, calls=%fused_computation.81 | loop fusion | flops 19660032 | bytes 22041600 | tf_op jit(solution)/shard_map/transpose(jvp())/reduce_sum | solution.py:162
  398.0 2.9 copy-done.40
  400.9 2.8 fusion.99
  403.8 9.9 %fusion.18 = (f32[8,12,128]{2,1,0:T(8,128)}, f32[8,12,128]{2,1,0:T(8,128)}, f32[8,128,128]{2,1,0:T(8,128)S(1)}) fusion(f32[8,128,128]{2,1,0:T(8,128)S(1)} %copy-done.93, f32[8,12,128]{2,1,0:T(8,128)S(1)} %fusion.198, pred[8,128,128]{2,1,0:T(8,128)(4,1)S(1)} %copy-done.113, f32[8,128,12,64]{1,0,3,2:T(8,128)S(1)} %bitcast.667, ...), kind=kOutput, calls=%fused_computation.37 | convolution fusion | flops 618766336 | bytes 7667712 | tf_op jit(solution)/shard_map/transpose(jvp(chij,chjp->chip))/dot_general | solution.py:120
  418.8 2.9 fusion.102
  422.4 3.7 multiply_reduce_fusion.21
  430.2 3.3 fusion.147
  433.6 4.7 fusion.36
  438.3 3.9 copy.227
  446.4 3.9 fusion.32
  454.4 2.2 fusion.78
  467.8 8.8 %fusion.239 = f32[1024,1024]{1,0:T(8,128)} fusion(f32[1024,1024]{1,0:T(8,128)S(1)} %copy-done.6, bf16[256,256]{0,1:T(8,128)(2,1)S(1)} %bitcast.734, bf16[256,256]{0,1:T(8,128)(2,1)S(1)} %bitcast.730, bf16[256,256]{0,1:T(8,128)(2,1)S(1)} %bitcast.728, bf16[256,256]{0,1:T(8,128)(2,1)S(1)} %bitcast.726, bf16[1024,768]{0,1:T(8,128)(2,1)S(1)} %copy-done.69), kind=kOutput, calls=%fused_computation.516 | convolution fusion | flops 2159017984 | bytes 10485760 | tf_op jit(solution)/shard_map/dot_general | solution.py:32
  476.6 11.7 %multiply_reduce_fusion.9 = (f32[768]{0:T(1024)}, f32[768]{0:T(1024)}, f32[768]{0:T(1024)}, f32[768]{0:T(1024)}, f32[768]{0:T(1024)}, /*index=5*/f32[1024,768]{0,1:T(8,128)}) fusion(f32[1021,768]{0,1:T(8,128)} %slice_bitcast_fusion.1, pred[1024]{0:T(1024)(128)(4,1)S(1)} %copy-done.173, f32[1024,2,768]{0,2,1:T(8,128)} %bitcast.654, ...), kind=kLoop, calls=%fused_computation.86 | loop fusion | flops 18084096 | bytes 25168896 | tf_op jit(solution)/shard_map/transpose(jvp())/reduce_sum | solution.py:96
  488.3 10.3 %reduce-scatter.4.cloned.1.call-done = f32[64,3072]{1,0:T(8,128)} async-done(((f32[1024,3072]{1,0:T(8,128)}), f32[64,3072]{1,0:T(8,128)}) %reduce-scatter.4.cloned.1.call-update) | async-done | bytes 786448 | tf_op jit(solution)/shard_map/reduce_scatter | solution.py:366
  516.6 2.1 copy-done.94
  518.7 8.2 fusion.150
  526.9 48.0 %reduce-scatter.6.cloned.1.call-done = f32[64,1024]{1,0:T(8,128)} async-done(((f32[1024,1024]{1,0:T(8,128)}), f32[64,1024]{1,0:T(8,128)}) %reduce-scatter.6.cloned.1.call-update) | async-done | bytes 262160 | tf_op jit(solution)/shard_map/reduce_scatter | solution.py:406
  575.2 5.7 fusion.97
  582.4 9.4 %fusion.286 = f32[1024,1024]{1,0:T(8,128)} fusion(bf16[1024,2304]{0,1:T(8,128)(2,1)S(1)} %copy-done.95, bf16[1024,2304]{1,0:T(8,128)(2,1)} %copy-done.96), kind=kOutput, calls=%fused_computation.546 | convolution fusion | flops 4831838208 | bytes 13631488 | tf_op jit(solution)/shard_map/dot_general | solution.py:26
  593.3 81.6 %collective-permute-done.2 = f32[1024,1024]{1,0:T(8,128)} collective-permute-done((f32[1024,1024]{1,0:T(8,128)}, f32[1024,1024]{1,0:T(8,128)}, u32[]{:S(2)}, u32[]{:S(2)}) %collective-permute-start.2) | collective-permute-done | bytes 4194336 | tf_op jit(solution)/shard_map/ppermute | solution.py:238
  674.9 7.2 fusion.5
  682.1 80.2 %collective-permute-done.5 = f32[1024,1024]{1,0:T(8,128)} collective-permute-done((f32[1024,1024]{1,0:T(8,128)}, f32[1024,1024]{1,0:T(8,128)}, u32[]{:S(2)}, u32[]{:S(2)}) %collective-permute-start.5) | collective-permute-done | bytes 4194336 | tf_op jit(solution)/shard_map/ppermute | solution.py:238
  762.3 4.9 multiply_reduce_fusion.1
  767.3 57.7 %psum.37 = f32[7972]{0:T(1024)S(1)} all-reduce(f32[7972]{0:T(1024)S(1)} %constant_dynamic-update-slice_fusion.15), channel_id=1, replica_groups=mesh['dp'=16,'tensor'=2] {'dp'}, use_global_device_ids=true, to_apply=%region_55.56 | all-reduce | flops 7972 | bytes 63776 | tf_op jit(solution)/shard_map/psum | solution.py:422
  825.5 8.4 psum.38
  836.5 8.1 multiply_add_fusion
  856.2 10.5 %all-reduce.52.cloned.1.call-done = f32[64,256]{1,0:T(8,128)} async-done(((f32[64,256]{1,0:T(8,128)}), f32[64,256]{1,0:T(8,128)}) %all-reduce.52.cloned.1.call-update) | async-done | bytes 65552 | tf_op jit(solution)/shard_map/psum | solution.py:432
  (772 shorter events, 158.5 us)
Async XLA Ops:
  7.2 240.4 %copy-start = (bf16[1024,1024]{1,0:T(8,128)(2,1)S(1)}, bf16[1024,1024]{1,0:T(8,128)(2,1)}, u32[]{:S(2)}) copy-start(bf16[1024,1024]{1,0:T(8,128)(2,1)} %param.53) | copy-start | bytes 6291460
  7.2 491.4 %reduce-scatter.4.cloned.1.call-start = ((), (), s32[]{:S(2)}) async-start(), calls=%async_computation.3 | async-start | bytes 13369344 | tf_op jit(solution)/shard_map/reduce_scatter | solution.py:366
  7.3 69.3 %copy-start.237 = (f32[32]{0:T(128)}, f32[32]{0:T(128)S(1)}, u32[]{:S(2)}) copy-start(f32[32]{0:T(128)S(1)} %multiply_exponential_fusion) | copy-start | bytes 388
  8.3 66.4 %copy-start.243 = (f32[7]{0:T(128)}, f32[7]{0:T(128)S(1)}, u32[]{:S(2)}) copy-start(f32[7]{0:T(128)S(1)} %convert_reduce_fusion) | copy-start | bytes 88
  17.3 16.1 %copy-start.239 = (f32[12]{0:T(128)}, f32[12]{0:T(128)S(1)}, u32[]{:S(2)}) copy-start(f32[12]{0:T(128)S(1)} %get-tuple-element.347) | copy-start | bytes 148
  17.3 20.1 %copy-start.241 = (f32[12]{0:T(128)}, f32[12]{0:T(128)S(1)}, u32[]{:S(2)}) copy-start(f32[12]{0:T(128)S(1)} %get-tuple-element.349) | copy-start | bytes 148
  37.9 69.5 %copy-start.147 = (f32[8,12]{1,0:T(8,128)}, f32[8,12]{1,0:T(8,128)S(1)}, u32[]{:S(2)}) copy-start(f32[8,12]{1,0:T(8,128)S(1)} %slice_reduce_fusion) | copy-start | bytes 1156
  38.1 36.5 %copy-start.186 = (f32[7,12]{1,0:T(8,128)}, f32[7,12]{1,0:T(8,128)S(1)}, u32[]{:S(2)}) copy-start(f32[7,12]{1,0:T(8,128)S(1)} %fusion.215) | copy-start | bytes 1012
  42.3 36.5 %copy-start.54 = (f32[1021,256]{1,0:T(8,128)}, f32[1021,256]{1,0:T(8,128)S(1)}, u32[]{:S(2)}) copy-start(f32[1021,256]{1,0:T(8,128)S(1)} %slice.705) | copy-start | bytes 3136516
  69.0 13.4 %copy-start.145 = (f32[1024]{0:T(1024)}, f32[1024]{0:T(1024)S(1)}, u32[]{:S(2)}) copy-start(f32[1024]{0:T(1024)S(1)} %fusion.227) | copy-start | bytes 12292
  69.0 13.4 %copy-start.215 = (f32[1,256]{1,0:T(1,128)}, f32[1,256]{1,0:T(1,128)S(1)}, u32[]{:S(2)}) copy-start(f32[1,256]{1,0:T(1,128)S(1)} %get-tuple-element.322) | copy-start | bytes 3076
  69.0 13.4 %copy-start.217 = (f32[1,256]{1,0:T(1,128)}, f32[1,256]{1,0:T(1,128)S(1)}, u32[]{:S(2)}) copy-start(f32[1,256]{1,0:T(1,128)S(1)} %get-tuple-element.323) | copy-start | bytes 3076
  69.0 13.4 %copy-start.219 = (f32[1,256]{1,0:T(1,128)}, f32[1,256]{1,0:T(1,128)S(1)}, u32[]{:S(2)}) copy-start(f32[1,256]{1,0:T(1,128)S(1)} %get-tuple-element.320) | copy-start | bytes 3076
  69.0 13.4 %copy-start.227 = (f32[1,256]{1,0:T(1,128)}, f32[1,256]{1,0:T(1,128)S(1)}, u32[]{:S(2)}) copy-start(f32[1,256]{1,0:T(1,128)S(1)} %get-tuple-element.321) | copy-start | bytes 3076
  69.7 9.0 %copy-start.56 = (f32[1022,256]{1,0:T(8,128)S(1)}, f32[1022,256]{1,0:T(8,128)}, u32[]{:S(2)}) copy-start(f32[1022,256]{1,0:T(8,128)} %slice.704) | copy-start | bytes 3139588
  69.7 9.0 %copy-start.58 = (f32[1023,256]{1,0:T(8,128)S(1)}, f32[1023,256]{1,0:T(8,128)}, u32[]{:S(2)}) copy-start(f32[1023,256]{1,0:T(8,128)} %slice.703) | copy-start | bytes 3142660
  78.1 15.9 %copy-start.77 = (bf16[1024,1,32]{0,2,1:T(8,128)(2,1)}, bf16[1024,1,32]{0,2,1:T(8,128)(2,1)S(1)}, u32[]{:S(2)}) copy-start(bf16[1024,1,32]{0,2,1:T(8,128)(2,1)S(1)} %get-tuple-element.311) | copy-start | bytes 196612
  104.7 17.6 %copy-start.18 = (f32[1024,768]{0,1:T(8,128)}, f32[1024,768]{0,1:T(8,128)S(1)}, u32[]{:S(2)}) copy-start(f32[1024,768]{0,1:T(8,128)S(1)} %get-tuple-element.283) | copy-start | bytes 9437188
  122.3 14.2 %copy-start.144 = (f32[768]{0:T(1024)S(1)}, f32[768]{0:T(1024)}, u32[]{:S(2)}) copy-start(f32[768]{0:T(1024)} %param.47) | copy-start | bytes 9220
  146.8 48.7 %collective-permute-start = (f32[512,1024]{1,0:T(8,128)S(1)}, f32[512,1024]{1,0:T(8,128)S(1)}, u32[]{:S(2)}, u32[]{:S(2)}) collective-permute-start(f32[512,1024]{1,0:T(8,128)S(1)} %fusion.143), channel_id=1, source_target_pairs={{0,1},{1,0},{2,3},{3,2},{4,5},{5,4},{6,7},{7,6},{8,9},{9,8},{10,11... | collective-permute-start | bytes 6291464 | tf_op jit(solution)/shard_map/ppermute | solution.py:238
  150.2 88.2 %collective-permute-start.1 = (f32[512,1024]{1,0:T(8,128)S(1)}, f32[512,1024]{1,0:T(8,128)}, u32[]{:S(2)}, u32[]{:S(2)}) collective-permute-start(f32[512,1024]{1,0:T(8,128)S(1)} %fusion.141), channel_id=1, source_target_pairs={{0,1},{1,0},{2,3},{3,2},{4,5},{5,4},{6,7},{7,6},{8,9},{9,8},{10,11... | collective-permute-start | bytes 6291464 | tf_op jit(solution)/shard_map/ppermute | solution.py:238
  241.6 56.3 %copy-start.12 = (f32[512,1024]{1,0:T(8,128)}, f32[512,1024]{1,0:T(8,128)S(1)}, u32[]{:S(2)}) copy-start(f32[512,1024]{1,0:T(8,128)S(1)} %get-tuple-element.271) | copy-start | bytes 6291460
  241.6 56.3 %copy-start.14 = (f32[512,1024]{1,0:T(8,128)}, f32[512,1024]{1,0:T(8,128)S(1)}, u32[]{:S(2)}) copy-start(f32[512,1024]{1,0:T(8,128)S(1)} %get-tuple-element.295) | copy-start | bytes 6291460
  241.6 56.3 %copy-start.190 = (f32[512]{0:T(512)}, f32[512]{0:T(512)S(1)}, u32[]{:S(2)}) copy-start(f32[512]{0:T(512)S(1)} %add_rsqrt_fusion.3) | copy-start | bytes 6148
  249.7 59.5 %copy-start.109 = (bf16[512,1024]{1,0:T(8,128)(2,1)}, bf16[512,1024]{1,0:T(8,128)(2,1)S(1)}, u32[]{:S(2)}) copy-start(bf16[512,1024]{1,0:T(8,128)(2,1)S(1)} %get-tuple-element.292) | copy-start | bytes 3145732
  252.2 47.1 %copy-start.62 = (f32[512,1024]{1,0:T(8,128)}, f32[512,1024]{1,0:T(8,128)S(1)}, u32[]{:S(2)}) copy-start(f32[512,1024]{1,0:T(8,128)S(1)} %fusion.67) | copy-start | bytes 6291460
  252.2 45.6 %collective-permute-start.3 = (f32[512,1024]{1,0:T(8,128)S(1)}, f32[512,1024]{1,0:T(8,128)S(1)}, u32[]{:S(2)}, u32[]{:S(2)}) collective-permute-start(f32[512,1024]{1,0:T(8,128)S(1)} %fusion.67), channel_id=1, source_target_pairs={{0,1},{1,0},{2,3},{3,2},{4,5},{5,4},{6,7},{7,6},{8,9},{9,8},{10,11... | collective-permute-start | bytes 6291464 | tf_op jit(solution)/shard_map/ppermute | solution.py:238
  254.0 45.3 %copy-start.188 = (f32[512]{0:T(512)}, f32[512]{0:T(512)S(1)}, u32[]{:S(2)}) copy-start(f32[512]{0:T(512)S(1)} %add_rsqrt_fusion.2) | copy-start | bytes 6148
  307.7 45.0 %collective-permute-start.4 = (f32[512,1024]{1,0:T(8,128)}, f32[512,1024]{1,0:T(8,128)}, u32[]{:S(2)}, u32[]{:S(2)}) collective-permute-start(f32[512,1024]{1,0:T(8,128)} %fusion.71), channel_id=1, source_target_pairs={{0,1},{1,0},{2,3},{3,2},{4,5},{5,4},{6,7},{7,6},{8,9},{9,8},{10,11... | collective-permute-start | bytes 6291464 | tf_op jit(solution)/shard_map/ppermute | solution.py:238
  322.1 34.8 %copy-start.13 = (f32[512,1024]{1,0:T(8,128)S(1)}, f32[512,1024]{1,0:T(8,128)}, u32[]{:S(2)}) copy-start(f32[512,1024]{1,0:T(8,128)} %copy-done.12) | copy-start | bytes 6291460
  322.1 34.8 %copy-start.15 = (f32[512,1024]{1,0:T(8,128)S(1)}, f32[512,1024]{1,0:T(8,128)}, u32[]{:S(2)}) copy-start(f32[512,1024]{1,0:T(8,128)} %copy-done.14) | copy-start | bytes 6291460
  322.1 34.8 %copy-start.63 = (f32[512,1024]{1,0:T(8,128)S(1)}, f32[512,1024]{1,0:T(8,128)}, u32[]{:S(2)}) copy-start(f32[512,1024]{1,0:T(8,128)} %copy-done.62) | copy-start | bytes 6291460
  322.1 34.8 %copy-start.189 = (f32[512]{0:T(512)S(1)}, f32[512]{0:T(512)}, u32[]{:S(2)}) copy-start(f32[512]{0:T(512)} %copy-done.188) | copy-start | bytes 6148
  322.1 34.8 %copy-start.191 = (f32[512]{0:T(512)S(1)}, f32[512]{0:T(512)}, u32[]{:S(2)}) copy-start(f32[512]{0:T(512)} %copy-done.190) | copy-start | bytes 6148
  322.1 34.8 %copy-start.230 = (f32[512]{0:T(512)S(1)}, f32[512]{0:T(512)}, u32[]{:S(2)}) copy-start(f32[512]{0:T(512)} %broadcast_multiply_fusion.4) | copy-start | bytes 6148
  362.9 212.0 %reduce-scatter.6.cloned.1.call-start = ((), (), s32[]{:S(2)}) async-start(), calls=%async_computation.4 | async-start | bytes 4456448 | tf_op jit(solution)/shard_map/reduce_scatter | solution.py:406
  377.3 9.3 %copy-start.154 = (f32[768]{0:T(1024)S(1)}, f32[768]{0:T(1024)}, u32[]{:S(2)}) copy-start(f32[768]{0:T(1024)} %mul.1197) | copy-start | bytes 9220
  377.3 9.3 %copy-start.199 = (f32[1024]{0:T(1024)S(1)}, f32[1024]{0:T(1024)}, u32[]{:S(2)}) copy-start(f32[1024]{0:T(1024)} %get-tuple-element.326) | copy-start | bytes 12292
  403.8 10.0 %copy-start.66 = (f32[1024,128]{1,0:T(8,128)S(1)}, f32[1024,128]{1,0:T(8,128)}, u32[]{:S(2)}) copy-start(f32[1024,128]{1,0:T(8,128)} %get-tuple-element.302) | copy-start | bytes 1572868
  403.8 10.3 %copy-start.51 = (f32[1024,128]{1,0:T(8,128)S(1)}, f32[1024,128]{1,0:T(8,128)}, u32[]{:S(2)}) copy-start(f32[1024,128]{1,0:T(8,128)} %get-tuple-element.301) | copy-start | bytes 1572868
  488.3 13.5 %copy-start.100 = (f32[1024,32]{0,1:T(8,128)S(1)}, f32[1024,32]{0,1:T(8,128)}, u32[]{:S(2)}) copy-start(f32[1024,32]{0,1:T(8,128)} %get-tuple-element.324) | copy-start | bytes 393220
  498.6 349.5 %reduce-scatter.8.cloned.1.call-start = ((), (), s32[]{:S(2)}) async-start(), calls=%async_computation.5 | async-start | bytes 10027008 | tf_op jit(solution)/shard_map/reduce_scatter | solution.py:408
  526.9 48.2 %copy-start.110 = (bf16[512,1024]{1,0:T(8,128)(2,1)S(1)}, bf16[512,1024]{1,0:T(8,128)(2,1)}, u32[]{:S(2)}) copy-start(bf16[512,1024]{1,0:T(8,128)(2,1)} %copy-done.109) | copy-start | bytes 3145732
  574.9 291.8 %all-reduce.52.cloned.1.call-start = ((), (), s32[]{:S(2)}) async-start(), calls=%async_computation.6 | async-start | bytes 131072 | tf_op jit(solution)/shard_map/psum | solution.py:432
  580.9 11.2 %copy-start.198 = (f32[768]{0:T(1024)S(1)}, f32[768]{0:T(1024)}, u32[]{:S(2)}) copy-start(f32[768]{0:T(1024)} %get-tuple-element.254) | copy-start | bytes 9220
  580.9 11.4 %copy-start.249 = (f32[256]{0:T(256)S(1)}, f32[256]{0:T(256)}, u32[]{:S(2)}) copy-start(f32[256]{0:T(256)} %get-tuple-element.242) | copy-start | bytes 3076
  580.9 11.4 %copy-start.250 = (f32[256]{0:T(256)S(1)}, f32[256]{0:T(256)}, u32[]{:S(2)}) copy-start(f32[256]{0:T(256)} %get-tuple-element.243) | copy-start | bytes 3076
  580.9 11.4 %copy-start.251 = (f32[256]{0:T(256)S(1)}, f32[256]{0:T(256)}, u32[]{:S(2)}) copy-start(f32[256]{0:T(256)} %get-tuple-element.244) | copy-start | bytes 3076
  580.9 11.4 %copy-start.252 = (f32[256]{0:T(256)S(1)}, f32[256]{0:T(256)}, u32[]{:S(2)}) copy-start(f32[256]{0:T(256)} %get-tuple-element.245) | copy-start | bytes 3076
  580.9 11.4 %copy-start.253 = (f32[256]{0:T(256)S(1)}, f32[256]{0:T(256)}, u32[]{:S(2)}) copy-start(f32[256]{0:T(256)} %get-tuple-element.246) | copy-start | bytes 3076
  580.9 11.4 %copy-start.206 = (f32[768]{0:T(1024)S(1)}, f32[768]{0:T(1024)}, u32[]{:S(2)}) copy-start(f32[768]{0:T(1024)} %get-tuple-element.237) | copy-start | bytes 9220
  580.9 11.4 %copy-start.205 = (f32[768]{0:T(1024)S(1)}, f32[768]{0:T(1024)}, u32[]{:S(2)}) copy-start(f32[768]{0:T(1024)} %get-tuple-element.238) | copy-start | bytes 9220
  580.9 11.5 %copy-start.204 = (f32[768]{0:T(1024)S(1)}, f32[768]{0:T(1024)}, u32[]{:S(2)}) copy-start(f32[768]{0:T(1024)} %get-tuple-element.239) | copy-start | bytes 9220
  580.9 11.5 %copy-start.203 = (f32[768]{0:T(1024)S(1)}, f32[768]{0:T(1024)}, u32[]{:S(2)}) copy-start(f32[768]{0:T(1024)} %get-tuple-element.240) | copy-start | bytes 9220
  581.0 11.5 %copy-start.202 = (f32[768]{0:T(1024)S(1)}, f32[768]{0:T(1024)}, u32[]{:S(2)}) copy-start(f32[768]{0:T(1024)} %get-tuple-element.241) | copy-start | bytes 9220
  581.0 11.5 %copy-start.259 = (f32[12]{0:T(128)S(1)}, f32[12]{0:T(128)}, u32[]{:S(2)}) copy-start(f32[12]{0:T(128)} %get-tuple-element.313) | copy-start | bytes 148
  581.0 12.2 %copy-start.255 = (f32[12]{0:T(128)S(1)}, f32[12]{0:T(128)}, u32[]{:S(2)}) copy-start(f32[12]{0:T(128)} %get-tuple-element.256) | copy-start | bytes 148
  581.0 93.9 %collective-permute-start.2 = (f32[1024,1024]{1,0:T(8,128)}, f32[1024,1024]{1,0:T(8,128)}, u32[]{:S(2)}, u32[]{:S(2)}) collective-permute-start(f32[1024,1024]{1,0:T(8,128)} %fusion.97), channel_id=1, source_target_pairs={{0,1},{1,0},{2,3},{3,2},{4,5},{5,4},{6,7},{7,6},{8,9},{9,8},{10,11... | collective-permute-start | bytes 12582920 | tf_op jit(solution)/shard_map/ppermute | solution.py:238
  591.8 170.5 %collective-permute-start.5 = (f32[1024,1024]{1,0:T(8,128)}, f32[1024,1024]{1,0:T(8,128)}, u32[]{:S(2)}, u32[]{:S(2)}) collective-permute-start(f32[1024,1024]{1,0:T(8,128)} %fusion.286), channel_id=1, source_target_pairs={{0,1},{1,0},{2,3},{3,2},{4,5},{5,4},{6,7},{7,6},{8,9},{9,8},{10,11... | collective-permute-start | bytes 12582920 | tf_op jit(solution)/shard_map/ppermute | solution.py:238
  593.3 169.0 %copy-start.25 = (bf16[1024,1024]{1,0:T(8,128)(2,1)S(1)}, bf16[1024,1024]{1,0:T(8,128)(2,1)}, u32[]{:S(2)}) copy-start(bf16[1024,1024]{1,0:T(8,128)(2,1)} %param.37) | copy-start | bytes 6291460
  682.1 85.1 %copy-start.197 = (f32[1024]{0:T(1024)S(1)}, f32[1024]{0:T(1024)}, u32[]{:S(2)}) copy-start(f32[1024]{0:T(1024)} %get-tuple-element.235) | copy-start | bytes 12292
  682.1 85.1 %copy-start.201 = (f32[1024]{0:T(1024)S(1)}, f32[1024]{0:T(1024)}, u32[]{:S(2)}) copy-start(f32[1024]{0:T(1024)} %get-tuple-element.233) | copy-start | bytes 12292
  682.1 85.1 %copy-start.207 = (f32[768]{0:T(1024)S(1)}, f32[768]{0:T(1024)}, u32[]{:S(2)}) copy-start(f32[768]{0:T(1024)} %get-tuple-element.229) | copy-start | bytes 9220
  836.5 9.3 %copy-start.98 = (f32[64,3072]{1,0:T(8,128)S(1)}, f32[64,3072]{1,0:T(8,128)}, u32[]{:S(2)}) copy-start(f32[64,3072]{1,0:T(8,128)} %reduce-scatter.4.cloned.1.call-done) | copy-start | bytes 2359300
  (218 other events, 728.7 us)
Sparse Core Ops, SparseCore 0:
  363.1 135.5 reduce-scatter.3
  503.0 71.8 reduce-scatter.5
  579.6 110.3 reduce-scatter.7
  849.8 16.8 all-reduce.51
